TPU v7x, 128 devices: a whole 4x4x4 slice. The times are simulated.
128 devices in a mesh: qblk: 16 (over x_lo, y, core), kblk: 8 (over z, x_hi).
Axes of the slice: x: 4 (x_hi: 2, x_lo: 2; x = x_hi * 2 + x_lo), y: 4, z: 4, core: 2. Of those that a mesh axis runs over, the one named last changes fastest.
Arguments:
- queries: bfloat16 [32768, 128], P(('qblk', 'kblk')), may hold values from -8 to 8
- keys: bfloat16 [32768, 128], P(('qblk', 'kblk')), may hold values from -8 to 8
- values: bfloat16 [32768, 128], P(('qblk', 'kblk')), may hold values from -6 to 6
- grad_out: bfloat16 [32768, 128], P(('qblk', 'kblk')), may hold values from -6 to 6
- key_blocks: int32 [256, 16], replicated, may hold values from 0 to 255, as said below
Outputs:
- attended: bfloat16 [32768, 128], P(('qblk', 'kblk'))
- query_grads: bfloat16 [32768, 128], P(('qblk', 'kblk'))
- key_grads: bfloat16 [32768, 128], P(('qblk', 'kblk'))
- value_grads: bfloat16 [32768, 128], P(('qblk', 'kblk'))
Inputs may be any that keep to these rules, and one draw needn't show every extreme that they name: `key_blocks`: row b lists 16 key block numbers, each at most b; its first entry is b itself; numbers may repeat within a row.
All inputs are finite; a program needn't handle non-finite values.
Results may differ from a plain program's by a relative error of at most 0.034.
Values may be sent and summed in bfloat16 or wider, within the bound.
A program may use at most 64 MiB of HBM per device.

v0:
```python
import math

import jax
import jax.numpy as jnp
from jax import lax
from jax.sharding import PartitionSpec as P

BLOCK = 128


masked_score = -1e30


def against(left, right):
    return lax.dot_general(
        left, right, (((1,), (1,)), ((), ())), preferred_element_type=jnp.float32
    )


def across(left, right):
    return lax.dot_general(
        left, right, (((0,), (0,)), ((), ())), preferred_element_type=jnp.float32
    )


def in_blocks(block_fn, row_count):
    block_rows = 512
    firsts = jnp.arange(row_count // block_rows, dtype=jnp.int32) * block_rows
    stacked = lax.map(lambda anchor: block_fn(anchor, block_rows), firsts)
    return jax.tree.map(lambda layer: layer.reshape((row_count,) + layer.shape[2:]), stacked)


def per_device(queries, keys, values, grad_out, key_blocks):
    own_rows, head_dim = queries.shape
    block_len = BLOCK
    key_groups = lax.axis_size("kblk")
    query_index = lax.axis_index("qblk")
    key_index = lax.axis_index("kblk")
    score_scale = 1.0 / math.sqrt(head_dim)
    query_all, grad_all = (
        lax.all_gather(queries, "qblk", axis=0, tiled=True),
        lax.all_gather(grad_out, "qblk", axis=0, tiled=True),
    )
    key_all, value_all = (
        lax.all_gather(keys, "kblk", axis=0, tiled=True),
        lax.all_gather(values, "kblk", axis=0, tiled=True),
    )
    query_count = query_all.shape[0]
    key_count = key_all.shape[0]
    query_line = jnp.arange(query_count, dtype=jnp.int32)
    query_pos = (query_line // own_rows * key_groups + key_index) * own_rows + query_line % own_rows
    key_pos = query_index * key_count + jnp.arange(key_count, dtype=jnp.int32)
    query_block_ids = query_pos[::block_len] // block_len
    key_block_ids = key_pos[::block_len] // block_len
    listed = jnp.take(key_blocks, query_block_ids, axis=0)
    block_allowed = jnp.any(listed[:, :, None] == key_block_ids[None, None, :], axis=1)

    def tile(first_row, row_count):
        rows_q = lax.dynamic_slice_in_dim(query_all, first_row, row_count, 0)
        positions = lax.dynamic_slice_in_dim(query_pos, first_row, row_count, 0)
        coarse = lax.dynamic_slice_in_dim(
            block_allowed, first_row // block_len, row_count // block_len, 0
        )
        fine_allowed = jnp.broadcast_to(
            coarse[:, None, :, None],
            (row_count // block_len, block_len, key_count // block_len, block_len),
        ).reshape(row_count, key_count)
        allowed = fine_allowed & (positions[:, None] >= key_pos[None, :])
        scores = against(rows_q, key_all) * score_scale
        return (scores, allowed)

    def local_stats(first_row, row_count):
        scores, allowed = tile(first_row, row_count)
        row_top = jnp.max(jnp.where(allowed, scores, masked_score), axis=1)
        row_total = jnp.sum(jnp.where(allowed, jnp.exp(scores - row_top[:, None]), 0.0), axis=1)
        return (row_top, row_total)

    row_top, row_total = in_blocks(local_stats, query_count)
    top_all = lax.pmax(row_top, "qblk")
    total_all = lax.psum(row_total * jnp.exp(row_top - top_all), "qblk")
    log_total = top_all + jnp.log(total_all)

    def block_fn(anchor, block_rows):
        scores, allowed = tile(anchor, block_rows)
        offsets = lax.dynamic_slice_in_dim(log_total, anchor, block_rows, 0)
        weights = jnp.where(allowed, jnp.exp(scores - offsets[:, None]), 0.0).astype(jnp.bfloat16)
        return jnp.dot(weights, value_all, preferred_element_type=jnp.float32)

    attended = lax.psum_scatter(
        in_blocks(block_fn, lax.axis_size("qblk") * own_rows),
        "qblk",
        scatter_dimension=0,
        tiled=True,
    ).astype(jnp.bfloat16)
    own_delta = jnp.sum(grad_out.astype(jnp.float32) * attended.astype(jnp.float32), axis=1)
    delta_all = lax.all_gather(own_delta, "qblk", axis=0, tiled=True)
    back_rows = 512

    def back_step(running, anchor):
        scores, allowed = tile(anchor, back_rows)
        offsets = lax.dynamic_slice_in_dim(log_total, anchor, back_rows, 0)
        deltas = lax.dynamic_slice_in_dim(delta_all, anchor, back_rows, 0)
        rows_q = lax.dynamic_slice_in_dim(query_all, anchor, back_rows, 0)
        rows_grad = lax.dynamic_slice_in_dim(grad_all, anchor, back_rows, 0)
        exact = jnp.where(allowed, jnp.exp(scores - offsets[:, None]), 0.0)
        weights = exact.astype(jnp.bfloat16)
        prob_grad = against(rows_grad, value_all)
        score_grad = (exact * (prob_grad - deltas[:, None])).astype(jnp.bfloat16)
        query_grad = jnp.dot(score_grad, key_all, preferred_element_type=jnp.float32)
        pair = jnp.concatenate([across(score_grad, rows_q), across(weights, rows_grad)], axis=1)
        return (running + pair, query_grad)

    firsts = jnp.arange(query_count // back_rows, dtype=jnp.int32) * back_rows
    start_sums = jnp.zeros((key_count, 2 * head_dim), jnp.float32)
    key_terms, query_terms = lax.scan(back_step, start_sums, firsts)
    query_terms = query_terms.reshape(query_count, head_dim)
    query_grads = (
        lax.psum_scatter(
            query_terms.astype(jnp.bfloat16), "qblk", scatter_dimension=0, tiled=True
        ).astype(jnp.float32)
        * score_scale
    ).astype(jnp.bfloat16)
    key_sums = lax.psum_scatter(
        key_terms.astype(jnp.bfloat16), "kblk", scatter_dimension=0, tiled=True
    ).astype(jnp.float32)
    key_grads = (key_sums[:, :head_dim] * score_scale).astype(jnp.bfloat16)
    value_grads = key_sums[:, head_dim:].astype(jnp.bfloat16)
    return (attended, query_grads, key_grads, value_grads)


def solution(mesh):
    in_specs = (
        P(("qblk", "kblk"), None),
        P(("qblk", "kblk"), None),
        P(("qblk", "kblk"), None),
        P(("qblk", "kblk"), None),
        P(),
    )
    out_specs = (
        P(("qblk", "kblk"), None),
        P(("qblk", "kblk"), None),
        P(("qblk", "kblk"), None),
        P(("qblk", "kblk"), None),
    )
    return jax.shard_map(
        per_device, mesh=mesh, in_specs=in_specs, out_specs=out_specs, check_vma=False
    )
```

profile of v0, /device:TPU:0, one launch (start us, length us, event | category | flops | bytes accessed | tf_op | source)
XLA Modules:
  0.0 763.2 jit_solution(1475753098275851121)
XLA Ops:
  10.0 40.3 %all_gather.16 = bf16[2048,128]{1,0:T(8,128)(2,1)} all-gather(bf16[256,128]{1,0:T(8,128)(2,1)} %param.12), channel_id=1, replica_groups=mesh['qblk'=16,'kblk'=8] {'kblk'}, dimensions={0}, use_global_device_ids=true | all-gather | bytes 589824 | tf_op jit(solution)/shard_map/all_gather | solution.py:45
  50.4 38.1 %all_gather.17 = bf16[2048,128]{1,0:T(8,128)(2,1)} all-gather(bf16[256,128]{1,0:T(8,128)(2,1)} %param.13), channel_id=1, replica_groups=mesh['qblk'=16,'kblk'=8] {'kblk'}, dimensions={0}, use_global_device_ids=true | all-gather | bytes 589824 | tf_op jit(solution)/shard_map/all_gather | solution.py:46
  88.4 104.4 %while.46 = (s32[]{:T(128)}, f32[8,512]{1,0:T(8,128)S(1)}, f32[8,512]{1,0:T(8,128)S(1)}, s32[8]{0:T(128)S(1)}, pred[32,16]{1,0:T(8,128)(4,1)S(1)}, /*index=5*/s3...) while((s32[]{:T(128)}, f32[8,512]{1,0:T(8,128)S(1)}, ...), condition=%wide.region_4.5_spmd.clone.clone, body=%wide.region_1.4_spmd.clone.sunk.clone | while | flops 279970848 | bytes 12237338 | solution.py:29
  93.4 4.4 select_reduce_fusion.6
  106.4 4.4 select_reduce_fusion.6
  119.5 4.4 select_reduce_fusion.6
  132.6 4.4 select_reduce_fusion.6
  145.6 4.4 select_reduce_fusion.6
  158.7 4.4 select_reduce_fusion.6
  171.7 4.4 select_reduce_fusion.6
  184.8 4.4 select_reduce_fusion.6
  192.9 53.1 %pmax.7 = f32[4096]{0:T(1024)S(1)} all-reduce(f32[4096]{0:T(1024)S(1)} %bitcast.129), channel_id=1, replica_groups=mesh['qblk'=16,'kblk'=8] {'qblk'}, use_global_device_ids=true, to_apply=%region_5.6 | all-reduce | flops 4096 | bytes 32768 | tf_op jit(solution)/shard_map/pmax | solution.py:79
  246.0 52.9 %psum.7 = f32[4096]{0:T(1024)S(1)} all-reduce(f32[4096]{0:T(1024)S(1)} %exponential_multiply_fusion), channel_id=1, replica_groups=mesh['qblk'=16,'kblk'=8] {'qblk'}, use_global_device_ids=true, to_apply=%region_6.7 | all-reduce | flops 4096 | bytes 32768 | tf_op jit(solution)/shard_map/psum | solution.py:80
  298.9 68.5 %while.47 = (s32[]{:T(128)}, f32[8,512,128]{2,1,0:T(8,128)}, s32[8]{0:T(128)S(1)}, pred[32,16]{1,0:T(8,128)(4,1)S(1)}, s32[4096]{0:T(1024)S(1)}, /*index=5*/bf16...) while((s32[]{:T(128)}, f32[8,512,128]{2,1,0:T(8,128)}, ...), condition=%wide.region_8.9_spmd.clone.clone, body=%wide.region_7.8_spmd.clone.sunk.clone | while | flops 543164416 | bytes 3568162 | solution.py:29
  321.1 3.5 fusion.89
  329.6 3.6 fusion.89
  346.8 3.6 fusion.89
  355.3 3.6 fusion.89
  363.9 3.6 fusion.89
  369.4 59.9 %reduce-scatter.4.cloned.1.call-done = f32[256,128]{1,0:T(8,128)} async-done(((f32[4096,128]{1,0:T(8,128)}), f32[256,128]{1,0:T(8,128)}) %reduce-scatter.4.cloned.1.call-update) | async-done | bytes 131088 | tf_op jit(solution)/shard_map/reduce_scatter | solution.py:89
  430.9 15.9 %all-gather = f32[16,1,256]{2,1,0:T(1,128)S(1)} all-gather(f32[1,1,256]{2,1,0:T(1,128)S(1)} %bitcast.135), channel_id=1, replica_groups=mesh['qblk'=16,'kblk'=8] {'qblk'}, dimensions={0}, use_global_device_ids=true | all-gather | bytes 17408 | tf_op jit(solution)/shard_map/all_gather | solution.py:96
  446.8 15.4 %all-gather.6.cloned.1.call-done = bf16[4096,128]{1,0:T(8,128)(2,1)} async-done(((bf16[256,128]{1,0:T(8,128)(2,1)}), bf16[4096,128]{1,0:T(8,128)(2,1)}) %all-gather.6.cloned.1.call-update) | async-done | bytes 1048592 | tf_op jit(solution)/shard_map/all_gather | solution.py:42
  462.2 155.8 %while.48 = (s32[]{:T(128)}, f32[2048,256]{0,1:T(8,128)}, bf16[8,512,128]{2,1,0:T(8,128)(2,1)}, s32[8]{0:T(128)S(1)}, pred[32,16]{1,0:T(8,128)(4,1)S(1)}, /*inde...) while((s32[]{:T(128)}, f32[2048,256]{0,1:T(8,128)}, ...), condition=%wide.region_12.13_spmd.clone.clone, body=%wide.region_11.12_spmd.clone.sunk.clone | while | flops 1353189376 | bytes 31754832 | solution.py:115
  494.6 3.7 maximum_add_fusion.3
  514.2 3.7 maximum_add_fusion.3
  533.7 3.7 maximum_add_fusion.3
  553.3 3.7 maximum_add_fusion.3
  572.9 3.7 maximum_add_fusion.3
  592.4 3.7 maximum_add_fusion.3
  612.0 3.7 maximum_add_fusion.3
  621.2 71.3 %reduce-scatter.8.cloned.1.call-done = bf16[256,256]{1,0:T(8,128)(2,1)} async-done(((bf16[2048,256]{1,0:T(8,128)(2,1)}), bf16[256,256]{1,0:T(8,128)(2,1)}) %reduce-scatter.8.cloned.1.call-update) | async-done | bytes 131088 | tf_op jit(solution)/shard_map/reduce_scatter | solution.py:123
  695.5 59.7 %reduce-scatter.6.cloned.1.call-done = bf16[256,128]{1,0:T(8,128)(2,1)} async-done(((bf16[4096,128]{1,0:T(8,128)(2,1)}), bf16[256,128]{1,0:T(8,128)(2,1)}) %reduce-scatter.6.cloned.1.call-update) | async-done | bytes 65552 | tf_op jit(solution)/shard_map/reduce_scatter | solution.py:118
  (253 shorter events, 169.1 us)
Async XLA Ops:
  7.2 81.3 %all-gather.4.cloned.1.call-start = ((), (), s32[]{:S(2)}) async-start(), calls=%async_computation.3 | async-start | bytes 1114112 | tf_op jit(solution)/shard_map/all_gather | solution.py:41
  7.9 421.4 %reduce-scatter.4.cloned.1.call-start = ((), (), s32[]{:S(2)}) async-start(), calls=%async_computation.4 | async-start | bytes 2228224 | tf_op jit(solution)/shard_map/reduce_scatter | solution.py:89
  298.9 130.4 %copy-start = (bf16[256,128]{1,0:T(8,128)(2,1)S(1)}, bf16[256,128]{1,0:T(8,128)(2,1)}, u32[]{:S(2)}) copy-start(bf16[256,128]{1,0:T(8,128)(2,1)} %param.14) | copy-start | bytes 196612
  367.5 94.7 %all-gather.6.cloned.1.call-start = ((), (), s32[]{:S(2)}) async-start(), calls=%async_computation.5 | async-start | bytes 1114112 | tf_op jit(solution)/shard_map/all_gather | solution.py:42
  368.2 324.3 %reduce-scatter.8.cloned.1.call-start = ((), (), s32[]{:S(2)}) async-start(), calls=%async_computation.7 | async-start | bytes 1179648 | tf_op jit(solution)/shard_map/reduce_scatter | solution.py:123
  620.6 134.6 %reduce-scatter.6.cloned.1.call-start = ((), (), s32[]{:S(2)}) async-start(), calls=%async_computation.6 | async-start | bytes 1114112 | tf_op jit(solution)/shard_map/reduce_scatter | solution.py:118
Sparse Core Ops, SparseCore 0:
  9.7 35.5 all-gather.3
  367.6 61.6 reduce-scatter.3
  431.1 31.1 all-gather.5
  620.7 71.7 reduce-scatter.7
  694.9 60.2 reduce-scatter.5
where the time goes:
time: 766 us; the launch traced here: 763 us
  waiting for transfers between devices  208 us (27%)
  blocking collectives  200 us (26%)
  matrix products  150 us (20%)
  loops' own time  94.6 us (12%)
  other arithmetic  63 us (8%)
  local copies, waits for them, and re-layouts  32.8 us (4%)
  between operations  13.9 us (2%)
    dot_general x24, matrix products, against(): lax.dot_general(left, right, (((1,), (1,)), ((), ())), preferred_element_...  72.3 us
    reduce_scatter x1, waiting for transfers between devices, per_device(): lax.psum_scatter(key_terms.astype(jnp.bfloat16), 'kblk', scatter_dimensio...  71.3 us
    another operation x2, loops' own time, in_blocks(): stacked = lax.map(lambda anchor: block_fn(anchor, block_rows), firsts)  63 us
    reduce_scatter x1, waiting for transfers between devices, per_device(): lax.psum_scatter(in_blocks(block_fn, lax.axis_size('qblk') * own_rows), '...  59.9 us
    reduce_scatter x1, waiting for transfers between devices, per_device(): lax.psum_scatter(query_terms.astype(jnp.bfloat16), 'qblk', scatter_dimens...  59.7 us
    pmax x1, blocking collectives, per_device(): top_all = lax.pmax(row_top, 'qblk')  53.1 us
    psum x1, blocking collectives, per_device(): total_all = lax.psum(row_total * jnp.exp(row_top - top_all), 'qblk')  52.9 us
    all_gather x1, blocking collectives, per_device(): lax.all_gather(keys, 'kblk', axis=0, tiled=True)  40.3 us
  transfers between devices with their start and end apart: 5, of which 4 were waited for; matrix products, arithmetic and copies ran while one was open for 1% of the time, Pallas kernels for 0%

commit v1 on v0

--- a/solution.py
+++ b/solution.py
@@ -1,14 +1,20 @@
+import functools
 import math
 
 import jax
 import jax.numpy as jnp
 from jax import lax
+from jax.experimental import pallas as pl
+from jax.experimental.pallas import tpu as pltpu
 from jax.sharding import PartitionSpec as P
 
 BLOCK = 128
-
+SLOTS = 64
+UNROLL = 4
+MESH = pl.DeviceIdType.MESH
 
 masked_score = -1e30
+LOG2E = 1.4426950408889634
 
 
 def against(left, right):
@@ -21,6 +27,392 @@
     return lax.dot_general(
         left, right, (((0,), (0,)), ((), ())), preferred_element_type=jnp.float32
     )
+
+
+def dot(left, right):
+    return jnp.dot(left, right, preferred_element_type=jnp.float32)
+
+
+KEY, QUERY, SAME_KEY, DIAGONAL, PERM, PERM_KEY, SAME_QUERY, KEY_END, QUERY_END = range(9)
+
+
+def iota(shape, dim):
+    return lax.broadcasted_iota(jnp.int32, shape, dim)
+
+
+def fiota(shape, dim):
+    return iota(shape, dim).astype(jnp.float32)
+
+
+def ones_where(cond):
+    return jnp.where(cond, 1.0, 0.0).astype(jnp.float32)
+
+
+def list_pairs(i, j, blocks_ref, table, slot_query):
+    own = blocks_ref[pl.ds(pl.multiple_of(i * 16, 16), 16), :]
+    key_of = iota((16, 32), 1)
+    key_ids = (key_of // 2) * 16 + 2 * j + key_of % 2
+    listed = jnp.zeros((16, 32), jnp.float32)
+    for n in range(16):
+        listed = jnp.maximum(listed, ones_where(own[:, n : n + 1] == key_ids))
+    unit = ones_where(iota((32, 32), 0) == iota((32, 32), 1))
+    pairs = against(unit, listed)
+    earlier_query = ones_where(iota((16, 16), 0) < iota((16, 16), 1))
+    earlier_key = ones_where(iota((32, 32), 1) < iota((32, 32), 0))
+    in_key = dot(pairs, earlier_query)
+    in_query = dot(earlier_key, pairs)
+    key_count = jnp.sum(pairs, axis=1, keepdims=True)
+    query_count = jnp.sum(pairs, axis=0, keepdims=True)
+    key_first = jnp.sum(in_query, axis=1, keepdims=True)
+    query_first = jnp.sum(in_key, axis=0, keepdims=True)
+    by_key = jnp.where(pairs > 0, key_first + in_key, -1.0)
+    by_query = jnp.where(pairs > 0, query_first + in_query, -1.0)
+    total = jnp.sum(jnp.sum(pairs, axis=1, keepdims=True), axis=0, keepdims=True)
+
+    lane = fiota((32, 128), 1)
+    keys = fiota((32, 128), 0)
+    id_col = (iota((32, 128), 0) // 2) * 16 + 2 * j + iota((32, 128), 0) % 2
+    zero = jnp.zeros((32, 128), jnp.float32)
+    rows = {n: zero for n in range(7)}
+    for q in range(16):
+        at_key = by_key[:, q : q + 1] == lane
+        at_query = by_query[:, q : q + 1] == lane
+        rows[KEY] += jnp.where(at_key, keys, 0.0)
+        rows[QUERY] += jnp.where(at_key, float(q), 0.0)
+        rows[SAME_KEY] += jnp.where(at_key, ones_where(in_key[:, q : q + 1] > 0), 0.0)
+        rows[DIAGONAL] += jnp.where(at_key & (id_col == 16 * i + q), 1.0, 0.0)
+        rows[PERM] += jnp.where(at_query, by_key[:, q : q + 1], 0.0)
+        rows[PERM_KEY] += jnp.where(at_query, keys, 0.0)
+        rows[SAME_QUERY] += jnp.where(at_query, ones_where(in_query[:, q : q + 1] > 0), 0.0)
+    most = {KEY: 31, QUERY: 15, SAME_KEY: 1, DIAGONAL: 1, PERM: SLOTS - 1, PERM_KEY: 31, SAME_QUERY: 1}
+    for n in range(7):
+        rows[n] = jnp.sum(rows[n], axis=0, keepdims=True)
+        table[n : n + 1, :] = jnp.clip(rows[n].astype(jnp.int32), 0, most[n])
+    key_end = jnp.where(key_count > 0, key_first + key_count, 0.0)
+    key_end = jnp.sum(jnp.where(keys == lane, key_end, 0.0), axis=0, keepdims=True)
+    table[KEY_END : KEY_END + 1, :] = jnp.clip(key_end.astype(jnp.int32), 0, SLOTS)
+    query_end = jnp.where(query_count > 0, query_first + query_count, 0.0)
+    table[QUERY_END : QUERY_END + 1, 0:16] = jnp.clip(query_end.astype(jnp.int32), 0, SLOTS)
+
+    query_row = jnp.where(fiota((1, 128), 1) < total, rows[QUERY], -1.0)
+    slot_query[...] = jnp.sum(
+        jnp.where(iota((SLOTS, 128), 0) == iota((SLOTS, 128), 1), query_row, 0.0),
+        axis=1,
+        keepdims=True,
+    )
+
+
+def most_pairs(blocks_ref):
+    lists = jnp.transpose(blocks_ref[...].astype(jnp.float32)).astype(jnp.int32)
+    groups = (lists // 2) % 8
+    counts = jnp.zeros((8, 256), jnp.float32)
+    group_of = iota((8, 256), 0)
+    for n in range(16):
+        fresh = jnp.ones((1, 256), jnp.float32)
+        for m in range(n):
+            fresh = jnp.where(lists[m : m + 1] == lists[n : n + 1], 0.0, fresh)
+        counts += jnp.where(groups[n : n + 1] == group_of, fresh, 0.0)
+    member = ones_where(iota((256, 16), 0) // 16 == iota((256, 16), 1))
+    return jnp.max(dot(counts, member))
+
+
+def kernel(
+    q_ref, k_ref, v_ref, g_ref, blocks_ref,
+    attended_ref, query_grads_ref, key_grads_ref, value_grads_ref, flag_ref,
+    kv, qg, table_v, table, slot_query, bias, probs, prob_grads, tops, totals, moments,
+    stats_out, stats, offsets, deltas, rounded, key_acc, query_acc,
+    sib_out, sib_in, y_out, y_in, x_out, x_in, z_out, z_in, h_out, h_in,
+    local_sem, kv_send, kv_recv, qg_send, qg_recv, st_send, st_recv, red_send, red_recv,
+):
+    i, j = lax.axis_index("qblk"), lax.axis_index("kblk")
+    core, y, x = i % 2, (i // 2) % 4, i // 8
+    h, z = j % 2, j // 2
+    scale = 1.0 / math.sqrt(BLOCK)
+
+    def sibling():
+        return (i + 1 - 2 * core, j)
+
+    def x_partner():
+        return ((i + 8) % 16, j)
+
+    def y_peer(d):
+        return (x * 8 + ((y + d) % 4) * 2 + core, j)
+
+    def h_partner():
+        return (i, j + 1 - 2 * h)
+
+    def z_peer(d):
+        return (i, ((z + d) % 4) * 2 + h)
+
+    def zh_peer(d):
+        return (i, ((z + d) % 4) * 2 + 1 - h)
+
+    loads = []
+    for n, (src, dst) in enumerate(
+        ((k_ref, kv.at[i, 0]), (v_ref, kv.at[i, 1]), (q_ref, qg.at[j, 0]), (g_ref, qg.at[j, 1]))
+    ):
+        loads.append(pltpu.make_async_copy(src, dst, local_sem.at[n]))
+        loads[-1].start()
+
+    peers = [sibling(), x_partner(), h_partner()]
+    peers += [y_peer(d) for d in (1, 2, 3)] + [z_peer(d) for d in (1, 2, 3)]
+    peers += [zh_peer(d) for d in (1, 2, 3)]
+    barrier = pltpu.get_barrier_semaphore()
+    for peer in peers:
+        pl.semaphore_signal(barrier, inc=1, device_id=peer, device_id_type=MESH)
+    pl.semaphore_wait(barrier, len(peers))
+    for load in loads:
+        load.wait()
+
+    def send(src, dst, sems, n, peer):
+        copy = pltpu.make_async_remote_copy(
+            src_ref=src, dst_ref=dst, send_sem=sems[0].at[n], recv_sem=sems[1].at[n],
+            device_id=peer, device_id_type=MESH,
+        )
+        copy.start()
+        return copy
+
+    kv_sems, qg_sems = (kv_send, kv_recv), (qg_send, qg_recv)
+    kv_x = send(kv.at[i], kv.at[i], kv_sems, 0, x_partner())
+    qg_h = send(qg.at[j], qg.at[j], qg_sems, 0, h_partner())
+    kv_y = [send(kv.at[i], kv.at[i], kv_sems, d, y_peer(d)) for d in (1, 3, 2)]
+    qg_z = [send(qg.at[j], qg.at[j], qg_sems, d, z_peer(d)) for d in (1, 3, 2)]
+    kv_sib = [send(kv.at[i], kv.at[i], kv_sems, 7, sibling())]
+
+    list_pairs(i, j, blocks_ref, table_v, slot_query)
+    to_smem = pltpu.make_async_copy(table_v, table, local_sem.at[4])
+    to_smem.start()
+    bias[0] = jnp.zeros((BLOCK, BLOCK), jnp.float32)
+    bias[1] = jnp.where(
+        iota((BLOCK, BLOCK), 0) <= iota((BLOCK, BLOCK), 1), 0.0, masked_score
+    ).astype(jnp.float32)
+    key_acc[0] = jnp.zeros((2, BLOCK, BLOCK), jnp.float32)
+    query_acc[0] = jnp.zeros((2, BLOCK, BLOCK), jnp.float32)
+
+    kv_x.wait_recv()
+    far = (i + 8) % 16
+    kv_far = [send(kv.at[far], kv.at[far], kv_sems, 3 + d, y_peer(d)) for d in (1, 3, 2)]
+    kv_sib.append(send(kv.at[far], kv.at[far], kv_sems, 8, sibling()))
+    qg_h.wait_recv()
+    other = j + 1 - 2 * h
+    qg_far = [send(qg.at[other], qg.at[other], qg_sems, 3 + d, z_peer(d)) for d in (1, 3, 2)]
+
+    flag_ref[...] = jnp.full((8, 128), most_pairs(blocks_ref), jnp.float32).astype(jnp.int32)
+
+    for n, d in enumerate((1, 3, 2)):
+        kv_y[n].wait_recv()
+        src = x * 8 + ((y - d + 4) % 4) * 2 + core
+        kv_sib.append(send(kv.at[src], kv.at[src], kv_sems, 8 + d, sibling()))
+    for n, d in enumerate((1, 3, 2)):
+        kv_far[n].wait_recv()
+        src = (1 - x) * 8 + ((y - d + 4) % 4) * 2 + core
+        kv_sib.append(send(kv.at[src], kv.at[src], kv_sems, 11 + d, sibling()))
+    for copy in qg_z + qg_far:
+        copy.wait_recv()
+    for copy in kv_sib:
+        copy.wait_recv()
+    to_smem.wait()
+
+    def score_step(step, carry):
+        for u in range(UNROLL):
+            s = step * UNROLL + u
+            k, q = table[KEY, s], table[QUERY, s]
+            scores = against(kv[k // 2, 0, k % 2], qg[q // 2, 0, q % 2]) * (scale * LOG2E)
+            scores += bias[table[DIAGONAL, s]]
+            prob_grad = against(kv[k // 2, 1, k % 2], qg[q // 2, 1, q % 2])
+            top = jnp.max(scores, axis=0, keepdims=True)
+            prob = jnp.exp2(scores - top)
+            probs[s] = prob
+            prob_grads[s] = prob_grad
+            tops[pl.ds(s, 1), :] = top
+            totals[pl.ds(s, 1), :] = jnp.sum(prob, axis=0, keepdims=True)
+            moments[pl.ds(s, 1), :] = jnp.sum(prob * prob_grad, axis=0, keepdims=True)
+        return carry
+
+    lax.fori_loop(0, SLOTS // UNROLL, score_step, 0)
+
+    top, total, moment, owner = tops[...], totals[...], moments[...], slot_query[...]
+    for q in range(16):
+        mine = owner == float(q)
+        top_q = jnp.max(jnp.where(mine, top, masked_score), axis=0, keepdims=True)
+        part = jnp.where(mine, jnp.exp2(top - top_q), 0.0)
+        total_q = jnp.sum(part * total, axis=0, keepdims=True)
+        moment_q = jnp.sum(part * moment, axis=0, keepdims=True)
+        some = total_q > 0
+        safe = jnp.where(some, total_q, 1.0)
+        stats_out[0, q : q + 1, :] = jnp.where(some, top_q + jnp.log2(safe), masked_score)
+        stats_out[1, q : q + 1, :] = moment_q / safe
+
+    st_sems = (st_send, st_recv)
+    st_copies = []
+    stats[j] = stats_out[...]
+    for n, peer in enumerate(
+        [z_peer(1), z_peer(3), h_partner(), z_peer(2), zh_peer(1), zh_peer(3), zh_peer(2)]
+    ):
+        st_copies.append(send(stats_out, stats.at[j], st_sems, n, peer))
+    for copy in st_copies:
+        copy.wait_recv()
+    logs = stats[:, 0]
+    best = jnp.max(logs, axis=0)
+    offset = best + jnp.log2(jnp.sum(jnp.exp2(logs - best[None]), axis=0))
+    delta = jnp.sum(jnp.exp2(logs - offset[None]) * stats[:, 1], axis=0)
+    for q in range(16):
+        offsets[q] = offset[q : q + 1, :]
+        deltas[q] = delta[q : q + 1, :]
+
+    def key_step(step, carry):
+        for u in range(UNROLL):
+            s = step * UNROLL + u
+            q = table[QUERY, s]
+            keep = table[SAME_KEY, s].astype(jnp.float32)
+            prob = probs[s] * jnp.exp2(tops[pl.ds(s, 1), :] - offsets[q])
+            weights = prob.astype(jnp.bfloat16)
+            score_grad = (prob * (prob_grads[s] - deltas[q])).astype(jnp.bfloat16)
+            rounded[s, 0] = score_grad
+            rounded[s, 1] = weights
+            key_acc[s + 1, 0] = key_acc[s, 0] * keep + dot(score_grad, qg[q // 2, 0, q % 2])
+            key_acc[s + 1, 1] = key_acc[s, 1] * keep + dot(weights, qg[q // 2, 1, q % 2])
+        return carry
+
+    lax.fori_loop(0, SLOTS // UNROLL, key_step, 0)
+
+    red = (red_send, red_recv)
+
+    def sib_step(n, carry):
+        owner = (n % 2) * 8 + (n // 2) * 2 + 1 - core
+        for b in range(2):
+            sib_out[n, :, b] = key_acc[table[KEY_END, owner * 2 + b]].astype(jnp.bfloat16)
+        return carry
+
+    lax.fori_loop(0, 8, sib_step, 0)
+    sib_copy = send(sib_out, sib_in, red, 0, sibling())
+
+    def query_step(step, carry):
+        for u in range(UNROLL):
+            s = step * UNROLL + u
+            k, at = table[PERM_KEY, s], table[PERM, s]
+            keep = table[SAME_QUERY, s].astype(jnp.float32)
+            query_acc[s + 1, 0] = query_acc[s, 0] * keep + across(rounded[at, 0], kv[k // 2, 0, k % 2])
+            query_acc[s + 1, 1] = query_acc[s, 1] * keep + across(rounded[at, 1], kv[k // 2, 1, k % 2])
+        return carry
+
+    lax.fori_loop(0, SLOTS // UNROLL, query_step, 0)
+
+    def z_step(n, carry):
+        for b in range(2):
+            z_out[n // 2, n % 2, :, b] = query_acc[table[QUERY_END, n * 2 + b]].astype(jnp.bfloat16)
+        return carry
+
+    lax.fori_loop(0, 8, z_step, 0)
+    z_copies = []
+    for d in (1, 3, 2):
+        z_copies.append(send(z_out.at[(z + d) % 4], z_in.at[d - 1], red, d, z_peer(d)))
+
+    sib_copy.wait_recv()
+
+    def y_step(n, carry):
+        owner = (n % 2) * 8 + (n // 2) * 2 + core
+        for b in range(2):
+            both = key_acc[table[KEY_END, owner * 2 + b]] + sib_in[n, :, b].astype(jnp.float32)
+            y_out[n // 2, n % 2, :, b] = both.astype(jnp.bfloat16)
+        return carry
+
+    lax.fori_loop(0, 8, y_step, 0)
+    y_copies = []
+    for d in (1, 3, 2):
+        y_copies.append(send(y_out.at[(y + d) % 4], y_in.at[d - 1], red, 3 + d, y_peer(d)))
+
+    def total_of(own, arrived, at):
+        total = own[at].astype(jnp.float32)
+        for d in range(3):
+            total += arrived[(d,) + at[1:]].astype(jnp.float32)
+        return total
+
+    def sum_of(own, arrived, row, col):
+        total = own[row, col].astype(jnp.float32)
+        for d in range(3):
+            total += arrived[d, col].astype(jnp.float32)
+        return total
+
+    for copy in z_copies:
+        copy.wait_recv()
+    h_out[...] = sum_of(z_out, z_in, z, 1 - h).astype(jnp.bfloat16)
+    h_copy = send(h_out, h_in, red, 7, h_partner())
+    for copy in y_copies:
+        copy.wait_recv()
+    x_out[...] = sum_of(y_out, y_in, y, 1 - x).astype(jnp.bfloat16)
+    x_copy = send(x_out, x_in, red, 8, x_partner())
+    query_sum = sum_of(z_out, z_in, z, h)
+    key_sum = sum_of(y_out, y_in, y, x)
+    h_copy.wait_recv()
+    query_sum += h_in[...].astype(jnp.float32)
+    for b in range(2):
+        rows = pl.ds(b * BLOCK, BLOCK)
+        query_grads_ref[rows, :] = (query_sum[0, b] * scale).astype(jnp.bfloat16)
+        attended_ref[rows, :] = query_sum[1, b].astype(jnp.bfloat16)
+    x_copy.wait_recv()
+    key_sum += x_in[...].astype(jnp.float32)
+    for b in range(2):
+        rows = pl.ds(b * BLOCK, BLOCK)
+        key_grads_ref[rows, :] = (key_sum[0, b] * scale).astype(jnp.bfloat16)
+        value_grads_ref[rows, :] = key_sum[1, b].astype(jnp.bfloat16)
+
+    for copy in [kv_x, qg_h, sib_copy, h_copy, x_copy]:
+        copy.wait_send()
+    for copy in kv_y + kv_far + kv_sib + qg_z + qg_far + st_copies + z_copies + y_copies:
+        copy.wait_send()
+
+
+def fast(queries, keys, values, grad_out, key_blocks):
+    rows, head = queries.shape
+    out = jax.ShapeDtypeStruct((rows, head), jnp.bfloat16)
+    f32, bf16 = jnp.float32, jnp.bfloat16
+    tile = (BLOCK, BLOCK)
+    dma = pltpu.SemaphoreType.DMA
+    any_spec = pl.BlockSpec(memory_space=pl.ANY)
+    vmem_spec = pl.BlockSpec(memory_space=pltpu.VMEM)
+    return pl.pallas_call(
+        kernel,
+        out_shape=[out] * 4 + [jax.ShapeDtypeStruct((8, 128), jnp.int32)],
+        in_specs=[any_spec] * 4 + [vmem_spec],
+        out_specs=[vmem_spec] * 5,
+        scratch_shapes=[
+            pltpu.VMEM((16, 2, 2) + tile, bf16),
+            pltpu.VMEM((8, 2, 2) + tile, bf16),
+            pltpu.VMEM((16, 128), jnp.int32),
+            pltpu.SMEM((16, 128), jnp.int32),
+            pltpu.VMEM((SLOTS, 1), f32),
+            pltpu.VMEM((2,) + tile, f32),
+            pltpu.VMEM((SLOTS,) + tile, f32),
+            pltpu.VMEM((SLOTS,) + tile, f32),
+            pltpu.VMEM((SLOTS, 128), f32),
+            pltpu.VMEM((SLOTS, 128), f32),
+            pltpu.VMEM((SLOTS, 128), f32),
+            pltpu.VMEM((2, 16, 128), f32),
+            pltpu.VMEM((8, 2, 16, 128), f32),
+            pltpu.VMEM((16, 1, 128), f32),
+            pltpu.VMEM((16, 1, 128), f32),
+            pltpu.VMEM((SLOTS, 2) + tile, bf16),
+            pltpu.VMEM((SLOTS + 1, 2) + tile, f32),
+            pltpu.VMEM((SLOTS + 1, 2) + tile, f32),
+            pltpu.VMEM((8, 2, 2) + tile, bf16),
+            pltpu.VMEM((8, 2, 2) + tile, bf16),
+            pltpu.VMEM((4, 2, 2, 2) + tile, bf16),
+            pltpu.VMEM((3, 2, 2, 2) + tile, bf16),
+            pltpu.VMEM((2, 2) + tile, bf16),
+            pltpu.VMEM((2, 2) + tile, bf16),
+            pltpu.VMEM((4, 2, 2, 2) + tile, bf16),
+            pltpu.VMEM((3, 2, 2, 2) + tile, bf16),
+            pltpu.VMEM((2, 2) + tile, bf16),
+            pltpu.VMEM((2, 2) + tile, bf16),
+            dma((5,)), dma((15,)), dma((15,)), dma((7,)), dma((7,)),
+            dma((7,)), dma((7,)), dma((9,)), dma((9,)),
+        ],
+        compiler_params=pltpu.CompilerParams(
+            collective_id=0, has_side_effects=True, vmem_limit_bytes=56 << 20
+        ),
+        name="block_sparse_attention",
+    )(*(x.reshape(2, BLOCK, BLOCK) for x in (queries, keys, values, grad_out)), key_blocks)
 
 
 def in_blocks(block_fn, row_count):
@@ -30,7 +422,7 @@
     return jax.tree.map(lambda layer: layer.reshape((row_count,) + layer.shape[2:]), stacked)
 
 
-def per_device(queries, keys, values, grad_out, key_blocks):
+def general(queries, keys, values, grad_out, key_blocks):
     own_rows, head_dim = queries.shape
     block_len = BLOCK
     key_groups = lax.axis_size("kblk")
@@ -128,20 +520,21 @@
     return (attended, query_grads, key_grads, value_grads)
 
 
+def per_device(queries, keys, values, grad_out, key_blocks):
+    *outs, most = fast(queries, keys, values, grad_out, key_blocks)
+    return lax.cond(
+        most[0, 0] > SLOTS,
+        lambda: general(queries, keys, values, grad_out, key_blocks),
+        lambda: tuple(outs),
+    )
+
+
 def solution(mesh):
-    in_specs = (
-        P(("qblk", "kblk"), None),
-        P(("qblk", "kblk"), None),
-        P(("qblk", "kblk"), None),
-        P(("qblk", "kblk"), None),
-        P(),
-    )
-    out_specs = (
-        P(("qblk", "kblk"), None),
-        P(("qblk", "kblk"), None),
-        P(("qblk", "kblk"), None),
-        P(("qblk", "kblk"), None),
-    )
+    split = P(("qblk", "kblk"), None)
     return jax.shard_map(
-        per_device, mesh=mesh, in_specs=in_specs, out_specs=out_specs, check_vma=False
-    )
+        per_device,
+        mesh=mesh,
+        in_specs=(split, split, split, split, P()),
+        out_specs=(split, split, split, split),
+        check_vma=False,
+    )

time: 766 us -> 84.9 us (0.11)
  waiting for transfers between devices: 208 us -> 0 us
  blocking collectives: 200 us -> 0 us
  matrix products: 150 us -> 0 us
  loops' own time: 94.6 us -> 0.23 us
  Pallas kernels: 0 us -> 64.6 us
  other arithmetic: 63 us -> 0 us
  local copies, waits for them, and re-layouts: 32.8 us -> 5.19 us
    reduce_scatter x3 -> x0, waiting for transfers between devices: 191 us -> none  [the longest x1 71.3 us: per_device(): lax.psum_scatter(key_terms.astype(jnp.bfloat16), 'kblk', scatter_dimensio...]
    dot_general x56 -> x0, matrix products: 150 us -> none  [the longest x24 72.3 us: against(): lax.dot_general(left, right, (((1,), (1,)), ((), ())), preferred_element_...]
    another operation x3 -> x1, loops' own time: 94.6 us -> 0.23 us  [per_device(): lax.cond(most[0, 0] > SLOTS, lambda: general(queries, keys, values, grad_...]
    all_gather x3 -> x0, blocking collectives: 94.4 us -> none  [the longest x1 40.3 us: per_device(): lax.all_gather(keys, 'kblk', axis=0, tiled=True)]
    pallas_call x0 -> x1, Pallas kernels: none -> 64.6 us  [fast(): pl.pallas_call(kernel, out_shape=[out] * 4 + [jax.ShapeDtypeStruct((8, 12...]
    pmax x1 -> x0, blocking collectives: 53.1 us -> none  [per_device(): top_all = lax.pmax(row_top, 'qblk')]
    psum x1 -> x0, blocking collectives: 52.9 us -> none  [per_device(): total_all = lax.psum(row_total * jnp.exp(row_top - top_all), 'qblk')]
    reduce_sum x9 -> x0, other arithmetic: 29.9 us -> none  [the longest x8 28.4 us: local_stats(): jnp.sum(jnp.where(allowed, jnp.exp(scores - row_top[:, None]), 0.0), axis=1)]
  transfers between devices with their start and end apart: 5 -> 0, of which waited for: 4 -> 0; matrix products, arithmetic and copies ran while one was open for 1% -> 0% of each run, Pallas kernels for 0% -> 0%
where the time goes in v1:
time: 84.9 us; the launch traced here: 84.7 us
  Pallas kernels  64.6 us (76%)
  between operations  14.7 us (17%)
  local copies, waits for them, and re-layouts  5.19 us (6%)
    pallas_call x1, Pallas kernels, fast(): pl.pallas_call(kernel, out_shape=[out] * 4 + [jax.ShapeDtypeStruct((8, 12...  64.6 us
    unnamed x5, local copies, waits for them, and re-layouts  3.99 us

profile of v1, /device:TPU:0, one launch (start us, length us, event | category | flops | bytes accessed | tf_op | source)
XLA Modules:
  0.0 84.7 jit_solution(13954720631774971030)
XLA Ops:
  7.2 1.5 %copy.44.blocks_ref = s32[256,16]{1,0:T(8,128)} copy(s32[256,16]{0,1:T(8,128)} %param.17) | data formatting | bytes 32768 | tf_op args[4]
  8.6 64.6 %block_sparse_attention.1 = (bf16[256,128]{1,0:T(8,128)(2,1)S(1)}, bf16[256,128]{1,0:T(8,128)(2,1)S(1)}, bf16[256,128]{1,0:T(8,128)(2,1)S(1)}, bf16[256,128]{1,0:T(8,128)(2,1)S(1)}, s32[8,128]{1,0:T(8,128)}) custom-call(bf16[2,128,128]{2,1,0:T(8,128)(2,1)} %bitcast.135, bf16[2,128,128]{2,1,0:T(8,128)(2,1)} %bitcast.133, bf16[2,128,128]{2,1,0:T(8,128)(2,1)} %bitcast.134, ...), custom_call_target="tpu_custom_call" | custom-call | tf_op jit(solution)/shard_map/block_sparse_attention/pallas_call | solution.py:374
  73.2 1.2 %slice.19 = s32[1,1]{1,0:T(1,128)} slice(s32[8,128]{1,0:T(8,128)} %get-tuple-element.436), slice={[0:1], [0:1]} | slice | bytes 8 | tf_op jit(solution)/shard_map/slice | solution.py:526
  75.1 0.2 conditional.1
  75.3 0.6 copy.131
  76.0 0.6 copy.132
  76.6 0.6 copy.133
  77.2 0.6 copy.134

commit v2 on v1

v2 whole, which is shorter than its diff:
```python
import functools
import math

import jax
import jax.numpy as jnp
from jax import lax
from jax.experimental import pallas as pl
from jax.experimental.pallas import tpu as pltpu
from jax.sharding import PartitionSpec as P

BLOCK = 128
SLOTS = 64
UNROLL = 4
MESH = pl.DeviceIdType.MESH

masked_score = -1e30
LOG2E = 1.4426950408889634


def against(left, right):
    return lax.dot_general(
        left, right, (((1,), (1,)), ((), ())), preferred_element_type=jnp.float32
    )


def across(left, right):
    return lax.dot_general(
        left, right, (((0,), (0,)), ((), ())), preferred_element_type=jnp.float32
    )


def dot(left, right):
    return jnp.dot(left, right, preferred_element_type=jnp.float32)


KEY, QUERY, SAME_KEY, DIAGONAL, PERM, PERM_KEY, SAME_QUERY, KEY_END, QUERY_END = range(9)
LISTED = 16


def iota(shape, dim):
    return lax.broadcasted_iota(jnp.int32, shape, dim)


def fiota(shape, dim):
    return iota(shape, dim).astype(jnp.float32)


def ones_where(cond):
    return jnp.where(cond, 1.0, 0.0).astype(jnp.float32)


def list_pairs(i, j, lists_ref, table, slot_query):
    lists = lists_ref[...].astype(jnp.float32)
    chosen = ones_where(iota((256, 16), 0) == 16 * i + iota((256, 16), 1))
    own = dot(lists, chosen)
    key_ids = ((iota((32, 16), 0) // 2) * 16 + 2 * j + iota((32, 16), 0) % 2).astype(jnp.float32)
    pairs = jnp.zeros((32, 16), jnp.float32)
    for n in range(16):
        pairs = jnp.maximum(pairs, ones_where(own[n : n + 1, :] == key_ids))
    earlier_query = ones_where(iota((16, 16), 0) < iota((16, 16), 1))
    earlier_key = ones_where(iota((32, 32), 1) < iota((32, 32), 0))
    in_key = dot(pairs, earlier_query)
    in_query = dot(earlier_key, pairs)
    key_count = jnp.sum(pairs, axis=1, keepdims=True)
    query_count = jnp.sum(pairs, axis=0, keepdims=True)
    key_first = jnp.sum(in_query, axis=1, keepdims=True)
    query_first = jnp.sum(in_key, axis=0, keepdims=True)
    by_key = jnp.where(pairs > 0, key_first + in_key, -1.0)
    by_query = jnp.where(pairs > 0, query_first + in_query, -1.0)
    total = jnp.sum(jnp.sum(pairs, axis=1, keepdims=True), axis=0, keepdims=True)

    lane = fiota((32, 128), 1)
    keys = fiota((32, 128), 0)
    id_col = (iota((32, 128), 0) // 2) * 16 + 2 * j + iota((32, 128), 0) % 2
    zero = jnp.zeros((32, 128), jnp.float32)
    rows = {n: zero for n in range(7)}
    for q in range(16):
        at_key = by_key[:, q : q + 1] == lane
        at_query = by_query[:, q : q + 1] == lane
        rows[KEY] += jnp.where(at_key, keys, 0.0)
        rows[QUERY] += jnp.where(at_key, float(q), 0.0)
        rows[SAME_KEY] += jnp.where(at_key, ones_where(in_key[:, q : q + 1] > 0), 0.0)
        rows[DIAGONAL] += jnp.where(at_key & (id_col == 16 * i + q), 1.0, 0.0)
        rows[PERM] += jnp.where(at_query, by_key[:, q : q + 1], 0.0)
        rows[PERM_KEY] += jnp.where(at_query, keys, 0.0)
        rows[SAME_QUERY] += jnp.where(at_query, ones_where(in_query[:, q : q + 1] > 0), 0.0)
    most = {KEY: 31, QUERY: 15, SAME_KEY: 1, DIAGONAL: 1, PERM: SLOTS - 1, PERM_KEY: 31, SAME_QUERY: 1}
    for n in range(7):
        rows[n] = jnp.sum(rows[n], axis=0, keepdims=True)
        table[n : n + 1, :] = jnp.clip(rows[n].astype(jnp.int32), 0, most[n])
    key_end = jnp.where(key_count > 0, key_first + key_count, 0.0)
    key_end = jnp.sum(jnp.where(keys == lane, key_end, 0.0), axis=0, keepdims=True)
    table[KEY_END : KEY_END + 1, :] = jnp.clip(key_end.astype(jnp.int32), 0, SLOTS)
    query_end = jnp.where(query_count > 0, query_first + query_count, 0.0)
    table[QUERY_END : QUERY_END + 1, 0:16] = jnp.clip(query_end.astype(jnp.int32), 0, SLOTS)
    if table.shape[0] > LISTED:
        table[LISTED : LISTED + 32, 0:16] = pairs.astype(jnp.int32)
        return

    query_row = jnp.where(fiota((1, 128), 1) < total, rows[QUERY], -1.0)
    slot_query[...] = jnp.sum(
        jnp.where(iota((SLOTS, 128), 0) == iota((SLOTS, 128), 1), query_row, 0.0),
        axis=1,
        keepdims=True,
    )


def most_pairs(lists_ref):
    lists = lists_ref[...]
    groups = (lists // 2) % 8
    counts = jnp.zeros((8, 256), jnp.float32)
    group_of = iota((8, 256), 0)
    for n in range(16):
        fresh = jnp.ones((1, 256), jnp.float32)
        for m in range(n):
            fresh = jnp.where(lists[m : m + 1] == lists[n : n + 1], 0.0, fresh)
        counts += jnp.where(groups[n : n + 1] == group_of, fresh, 0.0)
    member = ones_where(iota((256, 16), 0) // 16 == iota((256, 16), 1))
    return jnp.max(dot(counts, member))


class Refs:
    def __init__(self, names, refs):
        self.__dict__.update(zip(names, refs, strict=True))


def kernel(names, dense, *refs):
    r = Refs(names, refs)
    i, j = lax.axis_index("qblk"), lax.axis_index("kblk")
    core, y, x = i % 2, (i // 2) % 4, i // 8
    h, z = j % 2, j // 2
    scale = 1.0 / math.sqrt(BLOCK)
    kv, qg, table = r.kv, r.qg, r.table

    def sibling():
        return (i + 1 - 2 * core, j)

    def x_partner():
        return ((i + 8) % 16, j)

    def y_peer(d):
        return (x * 8 + ((y + d) % 4) * 2 + core, j)

    def h_partner():
        return (i, j + 1 - 2 * h)

    def z_peer(d):
        return (i, ((z + d) % 4) * 2 + h)

    def zh_peer(d):
        return (i, ((z + d) % 4) * 2 + 1 - h)

    loads = []
    for n, (src, dst) in enumerate(
        ((r.k, kv.at[i, 0]), (r.v, kv.at[i, 1]), (r.q, qg.at[j, 0]), (r.g, qg.at[j, 1]))
    ):
        loads.append(pltpu.make_async_copy(src, dst, r.local_sem.at[n]))
        loads[-1].start()

    peers = [sibling(), x_partner(), h_partner()]
    peers += [y_peer(d) for d in (1, 2, 3)] + [z_peer(d) for d in (1, 2, 3)]
    peers += [zh_peer(d) for d in (1, 2, 3)]
    barrier = pltpu.get_barrier_semaphore()
    for peer in peers:
        pl.semaphore_signal(barrier, inc=1, device_id=peer, device_id_type=MESH)
    pl.semaphore_wait(barrier, len(peers))
    for load in loads:
        load.wait()

    def send(src, dst, sems, n, peer):
        copy = pltpu.make_async_remote_copy(
            src_ref=src, dst_ref=dst, send_sem=sems[0].at[n], recv_sem=sems[1].at[n],
            device_id=peer, device_id_type=MESH,
        )
        copy.start()
        return copy

    kv_sems, qg_sems = (r.kv_send, r.kv_recv), (r.qg_send, r.qg_recv)
    kv_x = send(kv.at[i], kv.at[i], kv_sems, 0, x_partner())
    qg_h = send(qg.at[j], qg.at[j], qg_sems, 0, h_partner())
    kv_y = [send(kv.at[i], kv.at[i], kv_sems, d, y_peer(d)) for d in (1, 3, 2)]
    qg_z = [send(qg.at[j], qg.at[j], qg_sems, d, z_peer(d)) for d in (1, 3, 2)]
    kv_sib = [send(kv.at[i], kv.at[i], kv_sems, 7, sibling())]

    list_pairs(i, j, r.lists, r.table_v, None if dense else r.slot_query)
    to_smem = pltpu.make_async_copy(r.table_v, table, r.local_sem.at[4])
    to_smem.start()
    r.bias[0] = jnp.zeros((BLOCK, BLOCK), jnp.float32)
    r.bias[1] = jnp.where(
        iota((BLOCK, BLOCK), 0) <= iota((BLOCK, BLOCK), 1), 0.0, masked_score
    ).astype(jnp.float32)
    none = 0 if not dense else slice(None)
    r.key_acc[none] = jnp.zeros(r.key_acc[none].shape, jnp.float32)
    r.query_acc[none] = jnp.zeros(r.query_acc[none].shape, jnp.float32)

    kv_x.wait_recv()
    far = (i + 8) % 16
    kv_far = [send(kv.at[far], kv.at[far], kv_sems, 3 + d, y_peer(d)) for d in (1, 3, 2)]
    kv_sib.append(send(kv.at[far], kv.at[far], kv_sems, 8, sibling()))
    qg_h.wait_recv()
    other = j + 1 - 2 * h
    qg_far = [send(qg.at[other], qg.at[other], qg_sems, 3 + d, z_peer(d)) for d in (1, 3, 2)]

    if not dense:
        r.flag[0, 0] = most_pairs(r.lists)

    for n, d in enumerate((1, 3, 2)):
        kv_y[n].wait_recv()
        src = x * 8 + ((y - d + 4) % 4) * 2 + core
        kv_sib.append(send(kv.at[src], kv.at[src], kv_sems, 8 + d, sibling()))
    for n, d in enumerate((1, 3, 2)):
        kv_far[n].wait_recv()
        src = (1 - x) * 8 + ((y - d + 4) % 4) * 2 + core
        kv_sib.append(send(kv.at[src], kv.at[src], kv_sems, 11 + d, sibling()))
    for copy in qg_z + qg_far:
        copy.wait_recv()
    for copy in kv_sib:
        copy.wait_recv()
    to_smem.wait()

    (dense_stats if dense else slot_stats)(r, i, j, scale)

    st_sems = (r.st_send, r.st_recv)
    st_copies = []
    r.stats[j] = r.stats_out[...]
    for n, peer in enumerate(
        [z_peer(1), z_peer(3), h_partner(), z_peer(2), zh_peer(1), zh_peer(3), zh_peer(2)]
    ):
        st_copies.append(send(r.stats_out, r.stats.at[j], st_sems, n, peer))
    for copy in st_copies:
        copy.wait_recv()
    logs = r.stats[:, 0]
    best = jnp.max(logs, axis=0)
    offset = best + jnp.log2(jnp.sum(jnp.exp2(logs - best[None]), axis=0))
    delta = jnp.sum(jnp.exp2(logs - offset[None]) * r.stats[:, 1], axis=0)
    for q in range(16):
        r.offsets[q] = offset[q : q + 1, :]
        r.deltas[q] = delta[q : q + 1, :]

    (dense_key_grads if dense else slot_key_grads)(r, i, j, scale)

    def key_part(block):
        return r.key_acc[block if dense else table[KEY_END, block]]

    def query_part(block):
        return r.query_acc[block if dense else table[QUERY_END, block]]

    red = (r.red_send, r.red_recv)

    def sib_step(n, carry):
        owner = (n % 2) * 8 + (n // 2) * 2 + 1 - core
        for b in range(2):
            r.sib_out[n, :, b] = key_part(owner * 2 + b).astype(jnp.bfloat16)
        return carry

    lax.fori_loop(0, 8, sib_step, 0)
    sib_copy = send(r.sib_out, r.sib_in, red, 0, sibling())

    if not dense:
        slot_query_grads(r)

    def z_step(n, carry):
        for b in range(2):
            r.z_out[n // 2, n % 2, :, b] = query_part(n * 2 + b).astype(jnp.bfloat16)
        return carry

    lax.fori_loop(0, 8, z_step, 0)
    z_copies = []
    for d in (1, 3, 2):
        z_copies.append(send(r.z_out.at[(z + d) % 4], r.z_in.at[d - 1], red, d, z_peer(d)))

    sib_copy.wait_recv()

    def y_step(n, carry):
        owner = (n % 2) * 8 + (n // 2) * 2 + core
        for b in range(2):
            both = key_part(owner * 2 + b) + r.sib_in[n, :, b].astype(jnp.float32)
            r.y_out[n // 2, n % 2, :, b] = both.astype(jnp.bfloat16)
        return carry

    lax.fori_loop(0, 8, y_step, 0)
    y_copies = []
    for d in (1, 3, 2):
        y_copies.append(send(r.y_out.at[(y + d) % 4], r.y_in.at[d - 1], red, 3 + d, y_peer(d)))

    def sum_of(own, arrived, row, col):
        total = own[row, col].astype(jnp.float32)
        for d in range(3):
            total += arrived[d, col].astype(jnp.float32)
        return total

    for copy in z_copies:
        copy.wait_recv()
    r.h_out[...] = sum_of(r.z_out, r.z_in, z, 1 - h).astype(jnp.bfloat16)
    h_copy = send(r.h_out, r.h_in, red, 7, h_partner())
    for copy in y_copies:
        copy.wait_recv()
    r.x_out[...] = sum_of(r.y_out, r.y_in, y, 1 - x).astype(jnp.bfloat16)
    x_copy = send(r.x_out, r.x_in, red, 8, x_partner())
    query_sum = sum_of(r.z_out, r.z_in, z, h)
    key_sum = sum_of(r.y_out, r.y_in, y, x)
    h_copy.wait_recv()
    query_sum += r.h_in[...].astype(jnp.float32)
    for b in range(2):
        rows = pl.ds(b * BLOCK, BLOCK)
        r.query_grads[rows, :] = (query_sum[0, b] * scale).astype(jnp.bfloat16)
        r.attended[rows, :] = query_sum[1, b].astype(jnp.bfloat16)
    x_copy.wait_recv()
    key_sum += r.x_in[...].astype(jnp.float32)
    for b in range(2):
        rows = pl.ds(b * BLOCK, BLOCK)
        r.key_grads[rows, :] = (key_sum[0, b] * scale).astype(jnp.bfloat16)
        r.value_grads[rows, :] = key_sum[1, b].astype(jnp.bfloat16)

    for copy in [kv_x, qg_h, sib_copy, h_copy, x_copy]:
        copy.wait_send()
    for copy in kv_y + kv_far + kv_sib + qg_z + qg_far + st_copies + z_copies + y_copies:
        copy.wait_send()


def slot_stats(r, i, j, scale):
    kv, qg, table = r.kv, r.qg, r.table

    def step(n, carry):
        for u in range(UNROLL):
            s = n * UNROLL + u
            k, q = table[KEY, s], table[QUERY, s]
            scores = against(kv[k // 2, 0, k % 2], qg[q // 2, 0, q % 2]) * (scale * LOG2E)
            scores += r.bias[table[DIAGONAL, s]]
            prob_grad = against(kv[k // 2, 1, k % 2], qg[q // 2, 1, q % 2])
            top = jnp.max(scores, axis=0, keepdims=True)
            prob = jnp.exp2(scores - top)
            r.probs[s] = prob
            r.prob_grads[s] = prob_grad
            r.tops[pl.ds(s, 1), :] = top
            r.totals[pl.ds(s, 1), :] = jnp.sum(prob, axis=0, keepdims=True)
            r.moments[pl.ds(s, 1), :] = jnp.sum(prob * prob_grad, axis=0, keepdims=True)
        return carry

    lax.fori_loop(0, SLOTS // UNROLL, step, 0)

    top, total, moment, owner = r.tops[...], r.totals[...], r.moments[...], r.slot_query[...]
    for q in range(16):
        mine = owner == float(q)
        top_q = jnp.max(jnp.where(mine, top, masked_score), axis=0, keepdims=True)
        part = jnp.where(mine, jnp.exp2(top - top_q), 0.0)
        total_q = jnp.sum(part * total, axis=0, keepdims=True)
        moment_q = jnp.sum(part * moment, axis=0, keepdims=True)
        put_stats(r, q, top_q, total_q, moment_q)


def put_stats(r, q, top, total, moment):
    some = total > 0
    safe = jnp.where(some, total, 1.0)
    r.stats_out[0, pl.ds(q, 1), :] = jnp.where(some, top + jnp.log2(safe), masked_score)
    r.stats_out[1, pl.ds(q, 1), :] = moment / safe


def slot_key_grads(r, i, j, scale):
    def step(n, carry):
        for u in range(UNROLL):
            s = n * UNROLL + u
            q = r.table[QUERY, s]
            keep = r.table[SAME_KEY, s].astype(jnp.float32)
            prob = r.probs[s] * jnp.exp2(r.tops[pl.ds(s, 1), :] - r.offsets[q])
            weights = prob.astype(jnp.bfloat16)
            score_grad = (prob * (r.prob_grads[s] - r.deltas[q])).astype(jnp.bfloat16)
            r.rounded[s, 0] = score_grad
            r.rounded[s, 1] = weights
            r.key_acc[s + 1, 0] = r.key_acc[s, 0] * keep + dot(score_grad, r.qg[q // 2, 0, q % 2])
            r.key_acc[s + 1, 1] = r.key_acc[s, 1] * keep + dot(weights, r.qg[q // 2, 1, q % 2])
        return carry

    lax.fori_loop(0, SLOTS // UNROLL, step, 0)


def slot_query_grads(r):
    def step(n, carry):
        for u in range(UNROLL):
            s = n * UNROLL + u
            k, at = r.table[PERM_KEY, s], r.table[PERM, s]
            keep = r.table[SAME_QUERY, s].astype(jnp.float32)
            for m in range(2):
                new = across(r.rounded[at, m], r.kv[k // 2, m, k % 2])
                r.query_acc[s + 1, m] = r.query_acc[s, m] * keep + new
        return carry

    lax.fori_loop(0, SLOTS // UNROLL, step, 0)


def dense_tile(r, i, j, scale, q, k):
    scores = against(r.kv[k // 2, 0, k % 2], r.qg[q // 2, 0, q % 2]) * (scale * LOG2E)
    own = (k // 2) * 16 + 2 * j + k % 2 == 16 * i + q
    scores += r.bias[own.astype(jnp.int32)]
    prob_grad = against(r.kv[k // 2, 1, k % 2], r.qg[q // 2, 1, q % 2])
    listed = r.table[LISTED + k, q].astype(jnp.float32)
    return scores + (1.0 - listed) * masked_score, prob_grad, listed


def dense_stats(r, i, j, scale):
    def query_step(q, carry):
        def key_step(k, state):
            top, total, moment = state
            scores, prob_grad, listed = dense_tile(r, i, j, scale, q, k)
            higher = jnp.maximum(top, jnp.max(scores, axis=0, keepdims=True))
            prob = jnp.exp2(scores - higher) * listed
            shrink = jnp.exp2(top - higher)
            total = total * shrink + jnp.sum(prob, axis=0, keepdims=True)
            moment = moment * shrink + jnp.sum(prob * prob_grad, axis=0, keepdims=True)
            return higher, total, moment

        zero = jnp.zeros((1, BLOCK), jnp.float32)
        put_stats(r, q, *lax.fori_loop(0, 32, key_step, (zero + masked_score, zero, zero)))
        return carry

    lax.fori_loop(0, 16, query_step, 0)


def dense_key_grads(r, i, j, scale):
    def step(n, carry):
        q, k = n // 32, n % 32
        scores, prob_grad, listed = dense_tile(r, i, j, scale, q, k)
        prob = jnp.exp2(scores - r.offsets[q]) * listed
        weights = prob.astype(jnp.bfloat16)
        score_grad = (prob * (prob_grad - r.deltas[q])).astype(jnp.bfloat16)
        for m, left in enumerate((score_grad, weights)):
            r.key_acc[k, m] = r.key_acc[k, m] + dot(left, r.qg[q // 2, m, q % 2])
            r.query_acc[q, m] = r.query_acc[q, m] + across(left, r.kv[k // 2, m, k % 2])
        return carry

    lax.fori_loop(0, 16 * 32, step, 0)


def attention(dense, queries, keys, values, grad_out, lists):
    rows, head = queries.shape
    out = jax.ShapeDtypeStruct((rows, head), jnp.bfloat16)
    f32, bf16 = jnp.float32, jnp.bfloat16
    tile = (BLOCK, BLOCK)
    table_rows = LISTED + 32 if dense else LISTED
    dma = pltpu.SemaphoreType.DMA
    any_spec = pl.BlockSpec(memory_space=pl.ANY)
    vmem_spec = pl.BlockSpec(memory_space=pltpu.VMEM)
    smem_spec = pl.BlockSpec(memory_space=pltpu.SMEM)
    scratch = {
        "kv": pltpu.VMEM((16, 2, 2) + tile, bf16),
        "qg": pltpu.VMEM((8, 2, 2) + tile, bf16),
        "table_v": pltpu.VMEM((table_rows, 128), jnp.int32),
        "table": pltpu.SMEM((table_rows, 128), jnp.int32),
        "bias": pltpu.VMEM((2,) + tile, f32),
        "stats_out": pltpu.VMEM((2, 16, 128), f32),
        "stats": pltpu.VMEM((8, 2, 16, 128), f32),
        "offsets": pltpu.VMEM((16, 1, 128), f32),
        "deltas": pltpu.VMEM((16, 1, 128), f32),
        "key_acc": pltpu.VMEM((32 if dense else SLOTS + 1, 2) + tile, f32),
        "query_acc": pltpu.VMEM((16 if dense else SLOTS + 1, 2) + tile, f32),
        "sib_out": pltpu.VMEM((8, 2, 2) + tile, bf16),
        "sib_in": pltpu.VMEM((8, 2, 2) + tile, bf16),
        "y_out": pltpu.VMEM((4, 2, 2, 2) + tile, bf16),
        "y_in": pltpu.VMEM((3, 2, 2, 2) + tile, bf16),
        "x_out": pltpu.VMEM((2, 2) + tile, bf16),
        "x_in": pltpu.VMEM((2, 2) + tile, bf16),
        "z_out": pltpu.VMEM((4, 2, 2, 2) + tile, bf16),
        "z_in": pltpu.VMEM((3, 2, 2, 2) + tile, bf16),
        "h_out": pltpu.VMEM((2, 2) + tile, bf16),
        "h_in": pltpu.VMEM((2, 2) + tile, bf16),
        "local_sem": dma((5,)),
        "kv_send": dma((15,)),
        "kv_recv": dma((15,)),
        "qg_send": dma((7,)),
        "qg_recv": dma((7,)),
        "st_send": dma((7,)),
        "st_recv": dma((7,)),
        "red_send": dma((9,)),
        "red_recv": dma((9,)),
    }
    if not dense:
        scratch |= {
            "slot_query": pltpu.VMEM((SLOTS, 1), f32),
            "probs": pltpu.VMEM((SLOTS,) + tile, f32),
            "prob_grads": pltpu.VMEM((SLOTS,) + tile, f32),
            "tops": pltpu.VMEM((SLOTS, 128), f32),
            "totals": pltpu.VMEM((SLOTS, 128), f32),
            "moments": pltpu.VMEM((SLOTS, 128), f32),
            "rounded": pltpu.VMEM((SLOTS, 2) + tile, bf16),
        }
    outs = ["attended", "query_grads", "key_grads", "value_grads"] + ["flag"] * (not dense)
    out_shape, out_specs = [out] * 4, [vmem_spec] * 4
    if not dense:
        out_shape.append(jax.ShapeDtypeStruct((1, 1), f32))
        out_specs.append(smem_spec)
    return pl.pallas_call(
        functools.partial(kernel, ["q", "k", "v", "g", "lists"] + outs + list(scratch), dense),
        out_shape=out_shape,
        in_specs=[any_spec] * 4 + [vmem_spec],
        out_specs=out_specs,
        scratch_shapes=list(scratch.values()),
        compiler_params=pltpu.CompilerParams(
            collective_id=1 if dense else 0, has_side_effects=True, vmem_limit_bytes=56 << 20
        ),
        name="dense_attention" if dense else "block_sparse_attention",
    )(*(a.reshape(2, BLOCK, BLOCK) for a in (queries, keys, values, grad_out)), lists)


def per_device(queries, keys, values, grad_out, key_blocks):
    args = (queries, keys, values, grad_out, key_blocks.T)
    *outs, most = attention(False, *args)
    return lax.cond(
        most[0, 0] > SLOTS,
        lambda: tuple(attention(True, *args)),
        lambda: tuple(outs),
    )


def solution(mesh):
    split = P(("qblk", "kblk"), None)
    return jax.shard_map(
        per_device,
        mesh=mesh,
        in_specs=(split, split, split, split, P()),
        out_specs=(split, split, split, split),
        check_vma=False,
    )
```

time: 84.9 us -> 68.6 us (0.81)
  between operations: 14.7 us -> 1.41 us
  local copies, waits for them, and re-layouts: 5.19 us -> 2.54 us
    unnamed x5 -> x14, local copies, waits for them, and re-layouts: 3.99 us -> 2.54 us
    slice x1 -> x0, local copies, waits for them, and re-layouts: 1.2 us -> none  [per_device(): most[0, 0] > SLOTS]
where the time goes in v2:
time: 68.6 us; the launch traced here: 68.4 us
  Pallas kernels  64.5 us (94%)
  local copies, waits for them, and re-layouts  2.54 us (4%)
  between operations  1.41 us (2%)
    pallas_call x1, Pallas kernels, attention(): pl.pallas_call(functools.partial(kernel, ['q', 'k', 'v', 'g', 'lists'] +...  64.5 us
    unnamed x14, local copies, waits for them, and re-layouts  2.54 us

profile of v2, /device:TPU:0, one launch (start us, length us, event | category | flops | bytes accessed | tf_op | source)
XLA Modules:
  0.0 68.4 jit_solution(15288080714943228804)
XLA Ops:
  0.6 0.0 copy-start
  0.6 0.0 copy-start.1
  0.7 0.0 copy-start.2
  0.7 0.0 copy-start.3
  0.7 0.0 copy-start.4
  0.7 64.5 %block_sparse_attention.1 = (bf16[256,128]{1,0:T(8,128)(2,1)S(1)}, bf16[256,128]{1,0:T(8,128)(2,1)S(1)}, bf16[256,128]{1,0:T(8,128)(2,1)S(1)}, bf16[256,128]{1,0:T(8,128)(2,1)S(1)}, f32[1,1]{1,0:T(1,128)}) custom-call(bf16[2,128,128]{2,1,0:T(8,128)(2,1)} %bitcast.10, bf16[2,128,128]{2,1,0:T(8,128)(2,1)} %bitcast.12, bf16[2,128,128]{2,1,0:T(8,128)(2,1)} %bitcast.14, ...), custom_call_target="tpu_custom_call" | custom-call | tf_op jit(solution)/shard_map/block_sparse_attention/pallas_call | solution.py:491
  65.9 0.0 copy-done
  65.9 0.0 copy-done.1
  65.9 0.0 copy-done.2
  65.9 0.0 copy-done.3
  65.9 0.0 copy-done.4
  65.9 0.6 copy.29
  66.6 0.6 copy.30
  67.2 0.6 copy.31
  67.8 0.6 copy.32
  (1 shorter events, 0.0 us)
Async XLA Ops:
  0.6 65.2 %copy-start = (bf16[256,128]{1,0:T(8,128)(2,1)S(1)}, bf16[256,128]{1,0:T(8,128)(2,1)}, u32[]{:S(2)}) copy-start(bf16[256,128]{1,0:T(8,128)(2,1)} %param.7) | copy-start | bytes 196612
  0.6 65.2 %copy-start.1 = (bf16[256,128]{1,0:T(8,128)(2,1)S(1)}, bf16[256,128]{1,0:T(8,128)(2,1)}, u32[]{:S(2)}) copy-start(bf16[256,128]{1,0:T(8,128)(2,1)} %param.8) | copy-start | bytes 196612
  0.7 65.2 %copy-start.2 = (bf16[256,128]{1,0:T(8,128)(2,1)S(1)}, bf16[256,128]{1,0:T(8,128)(2,1)}, u32[]{:S(2)}) copy-start(bf16[256,128]{1,0:T(8,128)(2,1)} %param.9) | copy-start | bytes 196612
  0.7 65.2 %copy-start.3 = (bf16[256,128]{1,0:T(8,128)(2,1)S(1)}, bf16[256,128]{1,0:T(8,128)(2,1)}, u32[]{:S(2)}) copy-start(bf16[256,128]{1,0:T(8,128)(2,1)} %param.10) | copy-start | bytes 196612
  0.7 65.2 %copy-start.4 = (s32[256,16]{0,1:T(8,128)S(1)}, s32[256,16]{0,1:T(8,128)}, u32[]{:S(2)}) copy-start(s32[256,16]{0,1:T(8,128)} %param.11) | copy-start | bytes 49156

commit v3 on v2

--- a/solution.py
+++ b/solution.py
@@ -10,7 +10,7 @@
 
 BLOCK = 128
 SLOTS = 64
-UNROLL = 4
+UNROLL = 8
 MESH = pl.DeviceIdType.MESH
 
 masked_score = -1e30
@@ -36,6 +36,8 @@
 KEY, QUERY, SAME_KEY, DIAGONAL, PERM, PERM_KEY, SAME_QUERY, KEY_END, QUERY_END = range(9)
 LISTED = 16
 
+STAT_STEPS = ((False, 1), (False, -1), (True, 0), (False, 2), (True, 1), (True, -1), (True, 2))
+
 
 def iota(shape, dim):
     return lax.broadcasted_iota(jnp.int32, shape, dim)
@@ -49,9 +51,14 @@
     return jnp.where(cond, 1.0, 0.0).astype(jnp.float32)
 
 
+def query_id(i, j, q):
+    x = (i // 8 + j % 2 + (q // 2) % 2) % 2
+    return (x * 8 + i % 8) * 16 + q
+
+
 def list_pairs(i, j, lists_ref, table, slot_query):
     lists = lists_ref[...].astype(jnp.float32)
-    chosen = ones_where(iota((256, 16), 0) == 16 * i + iota((256, 16), 1))
+    chosen = ones_where(iota((256, 16), 0) == query_id(i, j, iota((256, 16), 1)))
     own = dot(lists, chosen)
     key_ids = ((iota((32, 16), 0) // 2) * 16 + 2 * j + iota((32, 16), 0) % 2).astype(jnp.float32)
     pairs = jnp.zeros((32, 16), jnp.float32)
@@ -80,7 +87,7 @@
         rows[KEY] += jnp.where(at_key, keys, 0.0)
         rows[QUERY] += jnp.where(at_key, float(q), 0.0)
         rows[SAME_KEY] += jnp.where(at_key, ones_where(in_key[:, q : q + 1] > 0), 0.0)
-        rows[DIAGONAL] += jnp.where(at_key & (id_col == 16 * i + q), 1.0, 0.0)
+        rows[DIAGONAL] += jnp.where(at_key & (id_col == query_id(i, j, q)), 1.0, 0.0)
         rows[PERM] += jnp.where(at_query, by_key[:, q : q + 1], 0.0)
         rows[PERM_KEY] += jnp.where(at_query, keys, 0.0)
         rows[SAME_QUERY] += jnp.where(at_query, ones_where(in_query[:, q : q + 1] > 0), 0.0)
@@ -115,8 +122,110 @@
         for m in range(n):
             fresh = jnp.where(lists[m : m + 1] == lists[n : n + 1], 0.0, fresh)
         counts += jnp.where(groups[n : n + 1] == group_of, fresh, 0.0)
-    member = ones_where(iota((256, 16), 0) // 16 == iota((256, 16), 1))
+    block = iota((256, 16), 0)
+    query_group = (block // 16 % 8) * 2 + (block // 128 + block // 2 % 2) % 2
+    member = ones_where(query_group == iota((256, 16), 1))
     return jnp.max(dot(counts, member))
+
+
+class Refs:
+    def __init__(self, names, refs):
+        self.__dict__.update(zip(names, refs, strict=True))
+
+
+def flip(bit):
+    return 1 - bit
+
+
+class Ring:
+    def __init__(self, a, p, peer, row, blocks, gather_sems, out, own_in, part_in, part_out, sum_out, sum_in, sum_sems):
+        self.a, self.p, self.peer, self.row = a, p, peer, row
+        self.blocks, self.gather_sems = blocks, gather_sems
+        self.out, self.own_in, self.part_in, self.part_out = out, own_in, part_in, part_out
+        self.sum_out, self.sum_in, self.sum_sems = sum_out, sum_in, sum_sems
+        self.copies = []
+
+    def at(self, step):
+        return (self.p + step + 4) % 4
+
+    def send(self, src, dst, sems, n, peer):
+        copy = pltpu.make_async_remote_copy(
+            src_ref=src, dst_ref=dst, send_sem=sems[0].at[n], recv_sem=sems[1].at[n],
+            device_id=peer, device_id_type=MESH,
+        )
+        copy.start()
+        self.copies.append(copy)
+        return copy
+
+    def pass_block(self, n, row, peer):
+        return self.send(self.blocks.at[row], self.blocks.at[row], self.gather_sems, n, peer)
+
+    def pass_half(self, n, row, half, peer):
+        ref = self.blocks.at[row, half]
+        return self.send(ref, ref, self.gather_sems, n, peer)
+
+    def start_own(self):
+        own = self.row(self.a, self.p)
+        self.to_pair = self.pass_block(0, own, self.peer(True, 0))
+        self.up = self.pass_block(1, own, self.peer(False, 1))
+        self.down = self.pass_block(2, own, self.peer(False, -1))
+
+    def start_far(self):
+        self.to_pair.wait_recv()
+        far = self.row(flip(self.a), self.p)
+        self.far_up = self.pass_block(5, far, self.peer(False, 1))
+        self.far_down = self.pass_block(6, far, self.peer(False, -1))
+        return far
+
+    def pass_on(self, n, arrived, step, a):
+        arrived.wait_recv()
+        row = self.row(a, self.at(step))
+        half = 0 if step < 0 else 1
+        return row, self.pass_half(n, row, half, self.peer(False, -step))
+
+    def start_sum(self, phase):
+        a = flip(self.a) if phase == 0 else self.a
+        n, out = 6 * phase, self.out
+        opposite = self.at(2)
+        self.part = [
+            self.send(out.at[a, opposite, 0], self.part_in.at[phase, 0], self.sum_sems, n, self.peer(False, 1)),
+            self.send(out.at[a, opposite, 1], self.part_in.at[phase, 1], self.sum_sems, n + 1, self.peer(False, -1)),
+        ]
+        plain = [
+            self.send(out.at[a, self.at(1), 1], self.own_in.at[phase, 1], self.sum_sems, n + 2, self.peer(False, 1)),
+            self.send(out.at[a, self.at(-1), 0], self.own_in.at[phase, 0], self.sum_sems, n + 3, self.peer(False, -1)),
+        ]
+        return [a, phase, self.part, plain, []]
+
+    def add_part(self, state):
+        a, phase, part, _, summed = state
+        n = 6 * phase + 4
+        for half, step in ((0, 1), (1, -1)):
+            part[half].wait_recv()
+            both = self.out[a, self.at(step), half].astype(jnp.float32) + self.part_in[phase, half].astype(jnp.float32)
+            self.part_out[phase, half] = both.astype(jnp.bfloat16)
+            summed.append(
+                self.send(
+                    self.part_out.at[phase, half], self.own_in.at[phase, 2 + half], self.sum_sems, n + half,
+                    self.peer(False, step),
+                )
+            )
+
+    def total(self, state):
+        a, phase, _, plain, summed = state
+        for copy in plain + summed:
+            copy.wait_recv()
+        total = self.out[a, self.p].astype(jnp.float32)
+        total += self.own_in[phase, 0:2].astype(jnp.float32)
+        return total + self.own_in[phase, 2:4].astype(jnp.float32)
+
+    def send_total(self, total):
+        self.sum_out[...] = total.astype(jnp.bfloat16)
+        self.across_pair = self.send(self.sum_out, self.sum_in, self.sum_sems, 12, self.peer(True, 0))
+
+    def other_total(self):
+        self.across_pair.wait_recv()
+        return self.sum_in[...].astype(jnp.float32)
 
 
 class Refs:
@@ -132,23 +241,20 @@
     scale = 1.0 / math.sqrt(BLOCK)
     kv, qg, table = r.kv, r.qg, r.table
 
-    def sibling():
-        return (i + 1 - 2 * core, j)
-
-    def x_partner():
-        return ((i + 8) % 16, j)
-
-    def y_peer(d):
-        return (x * 8 + ((y + d) % 4) * 2 + core, j)
-
-    def h_partner():
-        return (i, j + 1 - 2 * h)
-
-    def z_peer(d):
-        return (i, ((z + d) % 4) * 2 + h)
-
-    def zh_peer(d):
-        return (i, ((z + d) % 4) * 2 + 1 - h)
+    def key_row(x, y):
+        return x * 8 + y * 2 + core
+
+    def query_row(h, z):
+        return z * 2 + h
+
+    def key_peer(pair, step):
+        return (key_row(flip(x) if pair else x, (y + step + 4) % 4), j)
+
+    def query_peer(pair, step):
+        at = (z + step + 4) % 4
+        return ((i + 8) % 16, query_row(flip(h), at)) if pair else (i, query_row(h, at))
+
+    sibling = (i + 1 - 2 * core, j)
 
     loads = []
     for n, (src, dst) in enumerate(
@@ -157,9 +263,8 @@
         loads.append(pltpu.make_async_copy(src, dst, r.local_sem.at[n]))
         loads[-1].start()
 
-    peers = [sibling(), x_partner(), h_partner()]
-    peers += [y_peer(d) for d in (1, 2, 3)] + [z_peer(d) for d in (1, 2, 3)]
-    peers += [zh_peer(d) for d in (1, 2, 3)]
+    stat_peers = [query_peer(pair, step) for pair, step in STAT_STEPS]
+    peers = [sibling, key_peer(True, 0), key_peer(False, 1), key_peer(False, -1)] + stat_peers
     barrier = pltpu.get_barrier_semaphore()
     for peer in peers:
         pl.semaphore_signal(barrier, inc=1, device_id=peer, device_id_type=MESH)
@@ -167,24 +272,38 @@
     for load in loads:
         load.wait()
 
-    def send(src, dst, sems, n, peer):
-        copy = pltpu.make_async_remote_copy(
-            src_ref=src, dst_ref=dst, send_sem=sems[0].at[n], recv_sem=sems[1].at[n],
-            device_id=peer, device_id_type=MESH,
-        )
-        copy.start()
-        return copy
-
-    kv_sems, qg_sems = (r.kv_send, r.kv_recv), (r.qg_send, r.qg_recv)
-    kv_x = send(kv.at[i], kv.at[i], kv_sems, 0, x_partner())
-    qg_h = send(qg.at[j], qg.at[j], qg_sems, 0, h_partner())
-    kv_y = [send(kv.at[i], kv.at[i], kv_sems, d, y_peer(d)) for d in (1, 3, 2)]
-    qg_z = [send(qg.at[j], qg.at[j], qg_sems, d, z_peer(d)) for d in (1, 3, 2)]
-    kv_sib = [send(kv.at[i], kv.at[i], kv_sems, 7, sibling())]
+    keys = Ring(
+        x, y, key_peer, key_row, kv, (r.kv_send, r.kv_recv), r.key_out, r.key_own_in, r.key_part_in,
+        r.key_part_out, r.key_sum_out, r.key_sum_in, (r.key_send, r.key_recv),
+    )
+    queries = Ring(
+        h, z, query_peer, query_row, qg, (r.qg_send, r.qg_recv), r.query_out, r.query_own_in, r.query_part_in,
+        r.query_part_out, r.query_sum_out, r.query_sum_in, (r.query_send, r.query_recv),
+    )
+    sib = []
+
+    def to_sibling(ref):
+        sib.append(keys.send(ref, ref, (r.sib_send, r.sib_recv), len(sib), sibling))
+
+    keys.start_own()
+    queries.start_own()
+    to_sibling(kv.at[i])
 
     list_pairs(i, j, r.lists, r.table_v, None if dense else r.slot_query)
     to_smem = pltpu.make_async_copy(r.table_v, table, r.local_sem.at[4])
     to_smem.start()
+
+    to_sibling(kv.at[keys.start_far()])
+    queries.start_far()
+    far = (keys.far_down, keys.far_up), (queries.far_down, queries.far_up)
+    on = [], []
+    for ring, halves in ((keys, on[0]), (queries, on[1])):
+        for n, arrived, step in ((3, ring.up, -1), (4, ring.down, 1)):
+            row, copy = ring.pass_on(n, arrived, step, ring.a)
+            halves.append((copy, ring.row(ring.a, ring.at(2)), n - 3))
+            if ring is keys:
+                to_sibling(kv.at[row])
+
     r.bias[0] = jnp.zeros((BLOCK, BLOCK), jnp.float32)
     r.bias[1] = jnp.where(
         iota((BLOCK, BLOCK), 0) <= iota((BLOCK, BLOCK), 1), 0.0, masked_score
@@ -192,29 +311,21 @@
     none = 0 if not dense else slice(None)
     r.key_acc[none] = jnp.zeros(r.key_acc[none].shape, jnp.float32)
     r.query_acc[none] = jnp.zeros(r.query_acc[none].shape, jnp.float32)
-
-    kv_x.wait_recv()
-    far = (i + 8) % 16
-    kv_far = [send(kv.at[far], kv.at[far], kv_sems, 3 + d, y_peer(d)) for d in (1, 3, 2)]
-    kv_sib.append(send(kv.at[far], kv.at[far], kv_sems, 8, sibling()))
-    qg_h.wait_recv()
-    other = j + 1 - 2 * h
-    qg_far = [send(qg.at[other], qg.at[other], qg_sems, 3 + d, z_peer(d)) for d in (1, 3, 2)]
-
     if not dense:
         r.flag[0, 0] = most_pairs(r.lists)
 
-    for n, d in enumerate((1, 3, 2)):
-        kv_y[n].wait_recv()
-        src = x * 8 + ((y - d + 4) % 4) * 2 + core
-        kv_sib.append(send(kv.at[src], kv.at[src], kv_sems, 8 + d, sibling()))
-    for n, d in enumerate((1, 3, 2)):
-        kv_far[n].wait_recv()
-        src = (1 - x) * 8 + ((y - d + 4) % 4) * 2 + core
-        kv_sib.append(send(kv.at[src], kv.at[src], kv_sems, 11 + d, sibling()))
-    for copy in qg_z + qg_far:
-        copy.wait_recv()
-    for copy in kv_sib:
+    for ring, halves in ((keys, on[0]), (queries, on[1])):
+        for n, arrived, step in ((7, ring.far_up, -1), (8, ring.far_down, 1)):
+            row, copy = ring.pass_on(n, arrived, step, flip(ring.a))
+            halves.append((copy, ring.row(flip(ring.a), ring.at(2)), n - 7))
+            if ring is keys:
+                to_sibling(kv.at[row])
+    for ring, halves in ((keys, on[0]), (queries, on[1])):
+        for copy, row, half in halves:
+            copy.wait_recv()
+            if ring is keys:
+                to_sibling(kv.at[row, half])
+    for copy in sib:
         copy.wait_recv()
     to_smem.wait()
 
@@ -223,10 +334,8 @@
     st_sems = (r.st_send, r.st_recv)
     st_copies = []
     r.stats[j] = r.stats_out[...]
-    for n, peer in enumerate(
-        [z_peer(1), z_peer(3), h_partner(), z_peer(2), zh_peer(1), zh_peer(3), zh_peer(2)]
-    ):
-        st_copies.append(send(r.stats_out, r.stats.at[j], st_sems, n, peer))
+    for n, peer in enumerate(stat_peers):
+        st_copies.append(queries.send(r.stats_out, r.stats.at[j], st_sems, n, peer))
     for copy in st_copies:
         copy.wait_recv()
     logs = r.stats[:, 0]
@@ -245,76 +354,62 @@
     def query_part(block):
         return r.query_acc[block if dense else table[QUERY_END, block]]
 
-    red = (r.red_send, r.red_recv)
-
-    def sib_step(n, carry):
-        owner = (n % 2) * 8 + (n // 2) * 2 + 1 - core
-        for b in range(2):
-            r.sib_out[n, :, b] = key_part(owner * 2 + b).astype(jnp.bfloat16)
-        return carry
-
-    lax.fori_loop(0, 8, sib_step, 0)
-    sib_copy = send(r.sib_out, r.sib_in, red, 0, sibling())
+    swaps = []
+    for phase, at in ((0, flip(x)), (1, x)):
+
+        def sib_step(n, carry, phase=phase, at=at):
+            owner = at * 8 + n * 2 + 1 - core
+            for b in range(2):
+                r.sib_out[phase, n, :, b] = key_part(owner * 2 + b).astype(jnp.bfloat16)
+            return carry
+
+        lax.fori_loop(0, 4, sib_step, 0)
+        swaps.append(
+            keys.send(r.sib_out.at[phase], r.sib_in.at[phase], (r.sib_send, r.sib_recv), 10 + phase, sibling)
+        )
 
     if not dense:
         slot_query_grads(r)
 
-    def z_step(n, carry):
+    def query_out_step(n, carry):
         for b in range(2):
-            r.z_out[n // 2, n % 2, :, b] = query_part(n * 2 + b).astype(jnp.bfloat16)
+            r.query_out[n % 2, n // 2, :, b] = query_part(n * 2 + b).astype(jnp.bfloat16)
         return carry
 
-    lax.fori_loop(0, 8, z_step, 0)
-    z_copies = []
-    for d in (1, 3, 2):
-        z_copies.append(send(r.z_out.at[(z + d) % 4], r.z_in.at[d - 1], red, d, z_peer(d)))
-
-    sib_copy.wait_recv()
-
-    def y_step(n, carry):
-        owner = (n % 2) * 8 + (n // 2) * 2 + core
-        for b in range(2):
-            both = key_part(owner * 2 + b) + r.sib_in[n, :, b].astype(jnp.float32)
-            r.y_out[n // 2, n % 2, :, b] = both.astype(jnp.bfloat16)
-        return carry
-
-    lax.fori_loop(0, 8, y_step, 0)
-    y_copies = []
-    for d in (1, 3, 2):
-        y_copies.append(send(r.y_out.at[(y + d) % 4], r.y_in.at[d - 1], red, 3 + d, y_peer(d)))
-
-    def sum_of(own, arrived, row, col):
-        total = own[row, col].astype(jnp.float32)
-        for d in range(3):
-            total += arrived[d, col].astype(jnp.float32)
-        return total
-
-    for copy in z_copies:
-        copy.wait_recv()
-    r.h_out[...] = sum_of(r.z_out, r.z_in, z, 1 - h).astype(jnp.bfloat16)
-    h_copy = send(r.h_out, r.h_in, red, 7, h_partner())
-    for copy in y_copies:
-        copy.wait_recv()
-    r.x_out[...] = sum_of(r.y_out, r.y_in, y, 1 - x).astype(jnp.bfloat16)
-    x_copy = send(r.x_out, r.x_in, red, 8, x_partner())
-    query_sum = sum_of(r.z_out, r.z_in, z, h)
-    key_sum = sum_of(r.y_out, r.y_in, y, x)
-    h_copy.wait_recv()
-    query_sum += r.h_in[...].astype(jnp.float32)
+    lax.fori_loop(0, 8, query_out_step, 0)
+    query_sums = [queries.start_sum(0), queries.start_sum(1)]
+
+    key_sums = []
+    for phase, at in ((0, flip(x)), (1, x)):
+        swaps[phase].wait_recv()
+
+        def key_out_step(n, carry, phase=phase, at=at):
+            owner = at * 8 + n * 2 + core
+            for b in range(2):
+                both = key_part(owner * 2 + b) + r.sib_in[phase, n, :, b].astype(jnp.float32)
+                r.key_out[at, n, :, b] = both.astype(jnp.bfloat16)
+            return carry
+
+        lax.fori_loop(0, 4, key_out_step, 0)
+        key_sums.append(keys.start_sum(phase))
+
+    for phase in range(2):
+        queries.add_part(query_sums[phase])
+        keys.add_part(key_sums[phase])
+    queries.send_total(queries.total(query_sums[0]))
+    keys.send_total(keys.total(key_sums[0]))
+    query_total = queries.total(query_sums[1]) + queries.other_total()
     for b in range(2):
         rows = pl.ds(b * BLOCK, BLOCK)
-        r.query_grads[rows, :] = (query_sum[0, b] * scale).astype(jnp.bfloat16)
-        r.attended[rows, :] = query_sum[1, b].astype(jnp.bfloat16)
-    x_copy.wait_recv()
-    key_sum += r.x_in[...].astype(jnp.float32)
+        r.query_grads[rows, :] = (query_total[0, b] * scale).astype(jnp.bfloat16)
+        r.attended[rows, :] = query_total[1, b].astype(jnp.bfloat16)
+    key_total = keys.total(key_sums[1]) + keys.other_total()
     for b in range(2):
         rows = pl.ds(b * BLOCK, BLOCK)
-        r.key_grads[rows, :] = (key_sum[0, b] * scale).astype(jnp.bfloat16)
-        r.value_grads[rows, :] = key_sum[1, b].astype(jnp.bfloat16)
-
-    for copy in [kv_x, qg_h, sib_copy, h_copy, x_copy]:
-        copy.wait_send()
-    for copy in kv_y + kv_far + kv_sib + qg_z + qg_far + st_copies + z_copies + y_copies:
+        r.key_grads[rows, :] = (key_total[0, b] * scale).astype(jnp.bfloat16)
+        r.value_grads[rows, :] = key_total[1, b].astype(jnp.bfloat16)
+
+    for copy in keys.copies + queries.copies:
         copy.wait_send()
 
 
@@ -390,7 +485,7 @@
 
 def dense_tile(r, i, j, scale, q, k):
     scores = against(r.kv[k // 2, 0, k % 2], r.qg[q // 2, 0, q % 2]) * (scale * LOG2E)
-    own = (k // 2) * 16 + 2 * j + k % 2 == 16 * i + q
+    own = (k // 2) * 16 + 2 * j + k % 2 == query_id(i, j, q)
     scores += r.bias[own.astype(jnp.int32)]
     prob_grad = against(r.kv[k // 2, 1, k % 2], r.qg[q // 2, 1, q % 2])
     listed = r.table[LISTED + k, q].astype(jnp.float32)
@@ -453,26 +548,29 @@
         "deltas": pltpu.VMEM((16, 1, 128), f32),
         "key_acc": pltpu.VMEM((32 if dense else SLOTS + 1, 2) + tile, f32),
         "query_acc": pltpu.VMEM((16 if dense else SLOTS + 1, 2) + tile, f32),
-        "sib_out": pltpu.VMEM((8, 2, 2) + tile, bf16),
-        "sib_in": pltpu.VMEM((8, 2, 2) + tile, bf16),
-        "y_out": pltpu.VMEM((4, 2, 2, 2) + tile, bf16),
-        "y_in": pltpu.VMEM((3, 2, 2, 2) + tile, bf16),
-        "x_out": pltpu.VMEM((2, 2) + tile, bf16),
-        "x_in": pltpu.VMEM((2, 2) + tile, bf16),
-        "z_out": pltpu.VMEM((4, 2, 2, 2) + tile, bf16),
-        "z_in": pltpu.VMEM((3, 2, 2, 2) + tile, bf16),
-        "h_out": pltpu.VMEM((2, 2) + tile, bf16),
-        "h_in": pltpu.VMEM((2, 2) + tile, bf16),
+        "sib_out": pltpu.VMEM((2, 4, 2, 2) + tile, bf16),
+        "sib_in": pltpu.VMEM((2, 4, 2, 2) + tile, bf16),
         "local_sem": dma((5,)),
-        "kv_send": dma((15,)),
-        "kv_recv": dma((15,)),
-        "qg_send": dma((7,)),
-        "qg_recv": dma((7,)),
+        "kv_send": dma((9,)),
+        "kv_recv": dma((9,)),
+        "qg_send": dma((9,)),
+        "qg_recv": dma((9,)),
+        "sib_send": dma((12,)),
+        "sib_recv": dma((12,)),
         "st_send": dma((7,)),
         "st_recv": dma((7,)),
-        "red_send": dma((9,)),
-        "red_recv": dma((9,)),
     }
+    for ring in ("key", "query"):
+        scratch |= {
+            ring + "_out": pltpu.VMEM((2, 4, 2, 2) + tile, bf16),
+            ring + "_own_in": pltpu.VMEM((2, 4, 2) + tile, bf16),
+            ring + "_part_in": pltpu.VMEM((2, 2, 2) + tile, bf16),
+            ring + "_part_out": pltpu.VMEM((2, 2, 2) + tile, bf16),
+            ring + "_sum_out": pltpu.VMEM((2, 2) + tile, bf16),
+            ring + "_sum_in": pltpu.VMEM((2, 2) + tile, bf16),
+            ring + "_send": dma((13,)),
+            ring + "_recv": dma((13,)),
+        }
     if not dense:
         scratch |= {
             "slot_query": pltpu.VMEM((SLOTS, 1), f32),

time: 68.6 us -> 58.4 us (0.85)
  Pallas kernels: 64.5 us -> 54.2 us
    pallas_call x1, Pallas kernels: 64.5 us -> 54.2 us  [attention(): pl.pallas_call(functools.partial(kernel, ['q', 'k', 'v', 'g', 'lists'] +...]
where the time goes in v3:
time: 58.4 us; the launch traced here: 58.2 us
  Pallas kernels  54.2 us (93%)
  local copies, waits for them, and re-layouts  2.54 us (4%)
  between operations  1.41 us (2%)
    pallas_call x1, Pallas kernels, attention(): pl.pallas_call(functools.partial(kernel, ['q', 'k', 'v', 'g', 'lists'] +...  54.2 us
    unnamed x14, local copies, waits for them, and re-layouts  2.54 us

profile of v3, /device:TPU:0, one launch (start us, length us, event | category | flops | bytes accessed | tf_op | source)
XLA Modules:
  0.0 58.2 jit_solution(13105112831811632643)
XLA Ops:
  0.6 0.0 copy-start
  0.6 0.0 copy-start.1
  0.7 0.0 copy-start.2
  0.7 0.0 copy-start.3
  0.7 0.0 copy-start.4
  0.7 54.2 %block_sparse_attention.1 = (bf16[256,128]{1,0:T(8,128)(2,1)S(1)}, bf16[256,128]{1,0:T(8,128)(2,1)S(1)}, bf16[256,128]{1,0:T(8,128)(2,1)S(1)}, bf16[256,128]{1,0:T(8,128)(2,1)S(1)}, f32[1,1]{1,0:T(1,128)}) custom-call(bf16[2,128,128]{2,1,0:T(8,128)(2,1)} %bitcast.10, bf16[2,128,128]{2,1,0:T(8,128)(2,1)} %bitcast.12, bf16[2,128,128]{2,1,0:T(8,128)(2,1)} %bitcast.14, ...), custom_call_target="tpu_custom_call" | custom-call | tf_op jit(solution)/shard_map/block_sparse_attention/pallas_call | solution.py:589
  55.6 0.0 copy-done
  55.6 0.0 copy-done.1
  55.6 0.0 copy-done.2
  55.6 0.0 copy-done.3
  55.6 0.0 copy-done.4
  55.7 0.6 %copy.29 = bf16[256,128]{1,0:T(8,128)(2,1)} copy(bf16[256,128]{1,0:T(8,128)(2,1)S(1)} %get-tuple-element.61) | data formatting | bytes 131072
  56.3 0.6 %copy.30 = bf16[256,128]{1,0:T(8,128)(2,1)} copy(bf16[256,128]{1,0:T(8,128)(2,1)S(1)} %get-tuple-element.62) | data formatting | bytes 131072
  56.9 0.6 %copy.31 = bf16[256,128]{1,0:T(8,128)(2,1)} copy(bf16[256,128]{1,0:T(8,128)(2,1)S(1)} %get-tuple-element.63) | data formatting | bytes 131072
  57.5 0.6 %copy.32 = bf16[256,128]{1,0:T(8,128)(2,1)} copy(bf16[256,128]{1,0:T(8,128)(2,1)S(1)} %get-tuple-element.64) | data formatting | bytes 131072
  (1 shorter events, 0.0 us)
Async XLA Ops:
  0.6 55.0 %copy-start = (bf16[256,128]{1,0:T(8,128)(2,1)S(1)}, bf16[256,128]{1,0:T(8,128)(2,1)}, u32[]{:S(2)}) copy-start(bf16[256,128]{1,0:T(8,128)(2,1)} %param.7) | copy-start | bytes 196612
  0.6 55.0 %copy-start.1 = (bf16[256,128]{1,0:T(8,128)(2,1)S(1)}, bf16[256,128]{1,0:T(8,128)(2,1)}, u32[]{:S(2)}) copy-start(bf16[256,128]{1,0:T(8,128)(2,1)} %param.8) | copy-start | bytes 196612
  0.7 55.0 %copy-start.2 = (bf16[256,128]{1,0:T(8,128)(2,1)S(1)}, bf16[256,128]{1,0:T(8,128)(2,1)}, u32[]{:S(2)}) copy-start(bf16[256,128]{1,0:T(8,128)(2,1)} %param.9) | copy-start | bytes 196612
  0.7 55.0 %copy-start.3 = (bf16[256,128]{1,0:T(8,128)(2,1)S(1)}, bf16[256,128]{1,0:T(8,128)(2,1)}, u32[]{:S(2)}) copy-start(bf16[256,128]{1,0:T(8,128)(2,1)} %param.10) | copy-start | bytes 196612
  0.7 55.0 %copy-start.4 = (s32[256,16]{0,1:T(8,128)S(1)}, s32[256,16]{0,1:T(8,128)}, u32[]{:S(2)}) copy-start(s32[256,16]{0,1:T(8,128)} %param.11) | copy-start | bytes 49156

commit v4 on v3

--- a/solution.py
+++ b/solution.py
@@ -10,7 +10,7 @@
 
 BLOCK = 128
 SLOTS = 64
-UNROLL = 8
+UNROLL = 32
 MESH = pl.DeviceIdType.MESH
 
 masked_score = -1e30
@@ -157,45 +157,58 @@
         self.copies.append(copy)
         return copy
 
-    def pass_block(self, n, row, peer):
-        return self.send(self.blocks.at[row], self.blocks.at[row], self.gather_sems, n, peer)
-
     def pass_half(self, n, row, half, peer):
         ref = self.blocks.at[row, half]
         return self.send(ref, ref, self.gather_sems, n, peer)
 
     def start_own(self):
-        own = self.row(self.a, self.p)
-        self.to_pair = self.pass_block(0, own, self.peer(True, 0))
-        self.up = self.pass_block(1, own, self.peer(False, 1))
-        self.down = self.pass_block(2, own, self.peer(False, -1))
-
-    def start_far(self):
-        self.to_pair.wait_recv()
-        far = self.row(flip(self.a), self.p)
-        self.far_up = self.pass_block(5, far, self.peer(False, 1))
-        self.far_down = self.pass_block(6, far, self.peer(False, -1))
-        return far
-
-    def pass_on(self, n, arrived, step, a):
-        arrived.wait_recv()
-        row = self.row(a, self.at(step))
-        half = 0 if step < 0 else 1
-        return row, self.pass_half(n, row, half, self.peer(False, -step))
-
-    def start_sum(self, phase):
+        own, up, down = self.row(self.a, self.p), self.peer(False, 1), self.peer(False, -1)
+        self.gather = {0: self.pass_half(0, own, 0, self.peer(True, 0))}
+        self.gather[2] = self.pass_half(2, own, 0, up)
+        self.gather[4] = self.pass_half(4, own, 1, down)
+        self.gather[1] = self.pass_half(1, own, 1, self.peer(True, 0))
+        self.gather[3] = self.pass_half(3, own, 1, up)
+        self.gather[5] = self.pass_half(5, own, 0, down)
+
+    def gather_step(self, n):
+        self.gather[n].wait_recv()
+        up, down = self.peer(False, 1), self.peer(False, -1)
+        if n < 2:
+            row = self.row(flip(self.a), self.p)
+            if n == 0:
+                self.gather[8] = self.pass_half(8, row, 0, up)
+            else:
+                self.gather[10] = self.pass_half(10, row, 1, down)
+                self.gather[9] = self.pass_half(9, row, 1, up)
+                self.gather[11] = self.pass_half(11, row, 0, down)
+            return row, n
+        a = self.a if n < 8 else flip(self.a)
+        m = (n - 2) % 6
+        row = self.row(a, self.at((-1, -1, 1, 1, 2, 2)[m]))
+        half = (0, 1, 1, 0, 0, 1)[m]
+        if m == 0:
+            self.gather[n + 4] = self.pass_half(n + 4, row, half, up)
+        if m == 2:
+            self.gather[n + 3] = self.pass_half(n + 3, row, half, down)
+        return row, half
+
+    def start_part(self, phase):
         a = flip(self.a) if phase == 0 else self.a
-        n, out = 6 * phase, self.out
+        out, sems, n = self.out, self.sum_sems, 6 * phase
         opposite = self.at(2)
-        self.part = [
-            self.send(out.at[a, opposite, 0], self.part_in.at[phase, 0], self.sum_sems, n, self.peer(False, 1)),
-            self.send(out.at[a, opposite, 1], self.part_in.at[phase, 1], self.sum_sems, n + 1, self.peer(False, -1)),
+        part = [
+            self.send(out.at[a, opposite, 0], self.part_in.at[phase, 0], sems, n, self.peer(False, 1)),
+            self.send(out.at[a, opposite, 1], self.part_in.at[phase, 1], sems, n + 1, self.peer(False, -1)),
         ]
-        plain = [
-            self.send(out.at[a, self.at(1), 1], self.own_in.at[phase, 1], self.sum_sems, n + 2, self.peer(False, 1)),
-            self.send(out.at[a, self.at(-1), 0], self.own_in.at[phase, 0], self.sum_sems, n + 3, self.peer(False, -1)),
+        return [a, phase, part, [], []]
+
+    def start_plain(self, state):
+        a, phase, _, plain, _ = state
+        out, sems, n = self.out, self.sum_sems, 6 * phase
+        plain += [
+            self.send(out.at[a, self.at(1), 1], self.own_in.at[phase, 1], sems, n + 2, self.peer(False, 1)),
+            self.send(out.at[a, self.at(-1), 0], self.own_in.at[phase, 0], sems, n + 3, self.peer(False, -1)),
         ]
-        return [a, phase, self.part, plain, []]
 
     def add_part(self, state):
         a, phase, part, _, summed = state
@@ -282,27 +295,24 @@
     )
     sib = []
 
-    def to_sibling(ref):
+    def to_sibling(row, half):
+        ref = kv.at[row, half]
         sib.append(keys.send(ref, ref, (r.sib_send, r.sib_recv), len(sib), sibling))
+
+    def gather_steps(*steps):
+        for n in steps:
+            to_sibling(*keys.gather_step(n))
+            queries.gather_step(n)
 
     keys.start_own()
     queries.start_own()
-    to_sibling(kv.at[i])
+    to_sibling(i, 0)
+    to_sibling(i, 1)
 
     list_pairs(i, j, r.lists, r.table_v, None if dense else r.slot_query)
     to_smem = pltpu.make_async_copy(r.table_v, table, r.local_sem.at[4])
     to_smem.start()
-
-    to_sibling(kv.at[keys.start_far()])
-    queries.start_far()
-    far = (keys.far_down, keys.far_up), (queries.far_down, queries.far_up)
-    on = [], []
-    for ring, halves in ((keys, on[0]), (queries, on[1])):
-        for n, arrived, step in ((3, ring.up, -1), (4, ring.down, 1)):
-            row, copy = ring.pass_on(n, arrived, step, ring.a)
-            halves.append((copy, ring.row(ring.a, ring.at(2)), n - 3))
-            if ring is keys:
-                to_sibling(kv.at[row])
+    gather_steps(0, 2, 4, 1, 3, 5)
 
     r.bias[0] = jnp.zeros((BLOCK, BLOCK), jnp.float32)
     r.bias[1] = jnp.where(
@@ -314,17 +324,7 @@
     if not dense:
         r.flag[0, 0] = most_pairs(r.lists)
 
-    for ring, halves in ((keys, on[0]), (queries, on[1])):
-        for n, arrived, step in ((7, ring.far_up, -1), (8, ring.far_down, 1)):
-            row, copy = ring.pass_on(n, arrived, step, flip(ring.a))
-            halves.append((copy, ring.row(flip(ring.a), ring.at(2)), n - 7))
-            if ring is keys:
-                to_sibling(kv.at[row])
-    for ring, halves in ((keys, on[0]), (queries, on[1])):
-        for copy, row, half in halves:
-            copy.wait_recv()
-            if ring is keys:
-                to_sibling(kv.at[row, half])
+    gather_steps(8, 10, 9, 11, 6, 7, 12, 13)
     for copy in sib:
         copy.wait_recv()
     to_smem.wait()
@@ -365,49 +365,61 @@
 
         lax.fori_loop(0, 4, sib_step, 0)
         swaps.append(
-            keys.send(r.sib_out.at[phase], r.sib_in.at[phase], (r.sib_send, r.sib_recv), 10 + phase, sibling)
+            keys.send(r.sib_out.at[phase], r.sib_in.at[phase], (r.sib_send, r.sib_recv), 16 + phase, sibling)
         )
 
-    if not dense:
-        slot_query_grads(r)
-
-    def query_out_step(n, carry):
-        for b in range(2):
-            r.query_out[n % 2, n // 2, :, b] = query_part(n * 2 + b).astype(jnp.bfloat16)
-        return carry
-
-    lax.fori_loop(0, 8, query_out_step, 0)
-    query_sums = [queries.start_sum(0), queries.start_sum(1)]
-
-    key_sums = []
-    for phase, at in ((0, flip(x)), (1, x)):
+    def key_out(phase, at):
         swaps[phase].wait_recv()
 
-        def key_out_step(n, carry, phase=phase, at=at):
+        def step(n, carry):
             owner = at * 8 + n * 2 + core
             for b in range(2):
                 both = key_part(owner * 2 + b) + r.sib_in[phase, n, :, b].astype(jnp.float32)
                 r.key_out[at, n, :, b] = both.astype(jnp.bfloat16)
             return carry
 
-        lax.fori_loop(0, 4, key_out_step, 0)
-        key_sums.append(keys.start_sum(phase))
-
-    for phase in range(2):
-        queries.add_part(query_sums[phase])
-        keys.add_part(key_sums[phase])
+        lax.fori_loop(0, 4, step, 0)
+
+    def query_out(at):
+        def step(n, carry):
+            for b in range(2):
+                r.query_out[at, n, :, b] = query_part((n * 2 + at) * 2 + b).astype(jnp.bfloat16)
+            return carry
+
+        lax.fori_loop(0, 4, step, 0)
+
+    if not dense:
+        slot_query_grads(r, 0, SLOTS // 2)
+    key_out(0, flip(x))
+    key_sums = [keys.start_part(0)]
+    keys.start_plain(key_sums[0])
+    key_out(1, x)
+    key_sums.append(keys.start_part(1))
+    if not dense:
+        slot_query_grads(r, SLOTS // 2, SLOTS)
+    query_out(flip(h))
+    query_sums = [queries.start_part(0)]
+    queries.start_plain(query_sums[0])
+    keys.add_part(key_sums[0])
+    keys.start_plain(key_sums[1])
+    query_out(h)
+    query_sums.append(queries.start_part(1))
+    queries.add_part(query_sums[0])
+    queries.start_plain(query_sums[1])
+    keys.add_part(key_sums[1])
+    keys.send_total(keys.total(key_sums[0]))
+    queries.add_part(query_sums[1])
     queries.send_total(queries.total(query_sums[0]))
-    keys.send_total(keys.total(key_sums[0]))
+    key_total = keys.total(key_sums[1]) + keys.other_total()
+    for b in range(2):
+        rows = pl.ds(b * BLOCK, BLOCK)
+        r.key_grads[rows, :] = (key_total[0, b] * scale).astype(jnp.bfloat16)
+        r.value_grads[rows, :] = key_total[1, b].astype(jnp.bfloat16)
     query_total = queries.total(query_sums[1]) + queries.other_total()
     for b in range(2):
         rows = pl.ds(b * BLOCK, BLOCK)
         r.query_grads[rows, :] = (query_total[0, b] * scale).astype(jnp.bfloat16)
         r.attended[rows, :] = query_total[1, b].astype(jnp.bfloat16)
-    key_total = keys.total(key_sums[1]) + keys.other_total()
-    for b in range(2):
-        rows = pl.ds(b * BLOCK, BLOCK)
-        r.key_grads[rows, :] = (key_total[0, b] * scale).astype(jnp.bfloat16)
-        r.value_grads[rows, :] = key_total[1, b].astype(jnp.bfloat16)
 
     for copy in keys.copies + queries.copies:
         copy.wait_send()
@@ -469,10 +481,10 @@
     lax.fori_loop(0, SLOTS // UNROLL, step, 0)
 
 
-def slot_query_grads(r):
+def slot_query_grads(r, first, last):
     def step(n, carry):
         for u in range(UNROLL):
-            s = n * UNROLL + u
+            s = first + n * UNROLL + u
             k, at = r.table[PERM_KEY, s], r.table[PERM, s]
             keep = r.table[SAME_QUERY, s].astype(jnp.float32)
             for m in range(2):
@@ -480,7 +492,7 @@
                 r.query_acc[s + 1, m] = r.query_acc[s, m] * keep + new
         return carry
 
-    lax.fori_loop(0, SLOTS // UNROLL, step, 0)
+    lax.fori_loop(0, (last - first) // UNROLL, step, 0)
 
 
 def dense_tile(r, i, j, scale, q, k):
@@ -551,12 +563,12 @@
         "sib_out": pltpu.VMEM((2, 4, 2, 2) + tile, bf16),
         "sib_in": pltpu.VMEM((2, 4, 2, 2) + tile, bf16),
         "local_sem": dma((5,)),
-        "kv_send": dma((9,)),
-        "kv_recv": dma((9,)),
-        "qg_send": dma((9,)),
-        "qg_recv": dma((9,)),
-        "sib_send": dma((12,)),
-        "sib_recv": dma((12,)),
+        "kv_send": dma((14,)),
+        "kv_recv": dma((14,)),
+        "qg_send": dma((14,)),
+        "qg_recv": dma((14,)),
+        "sib_send": dma((18,)),
+        "sib_recv": dma((18,)),
         "st_send": dma((7,)),
         "st_recv": dma((7,)),
     }
@@ -599,13 +611,36 @@
     )(*(a.reshape(2, BLOCK, BLOCK) for a in (queries, keys, values, grad_out)), lists)
 
 
+def hand_out_kernel(*refs):
+    sems = refs[-1]
+    copies = [pltpu.make_async_copy(refs[n], refs[4 + n], sems.at[n]) for n in range(4)]
+    for copy in copies:
+        copy.start()
+    for copy in copies:
+        copy.wait()
+
+
+def hand_out(outs):
+    spec = pl.BlockSpec(memory_space=pl.ANY)
+    return tuple(
+        pl.pallas_call(
+            hand_out_kernel,
+            out_shape=[jax.ShapeDtypeStruct(out.shape, out.dtype) for out in outs],
+            in_specs=[spec] * 4,
+            out_specs=[spec] * 4,
+            scratch_shapes=[pltpu.SemaphoreType.DMA((4,))],
+            name="hand_out",
+        )(*outs)
+    )
+
+
 def per_device(queries, keys, values, grad_out, key_blocks):
     args = (queries, keys, values, grad_out, key_blocks.T)
     *outs, most = attention(False, *args)
     return lax.cond(
         most[0, 0] > SLOTS,
-        lambda: tuple(attention(True, *args)),
-        lambda: tuple(outs),
+        lambda: hand_out(attention(True, *args)),
+        lambda: hand_out(outs),
     )
 
 

time: 58.4 us -> 53.7 us (0.920)
  local copies, waits for them, and re-layouts: 2.54 us -> 0.02 us
  Pallas kernels: 54.2 us -> 51.7 us
    pallas_call x1, Pallas kernels: 54.2 us -> 50.9 us  [attention(): pl.pallas_call(functools.partial(kernel, ['q', 'k', 'v', 'g', 'lists'] +...]
    unnamed x14 -> x10, local copies, waits for them, and re-layouts: 2.54 us -> 0.02 us
    pallas_call x0 -> x1, Pallas kernels: none -> 0.73 us  [hand_out(): pl.pallas_call(hand_out_kernel, out_shape=[jax.ShapeDtypeStruct(out.shape...]
where the time goes in v4:
time: 53.7 us; the launch traced here: 53.1 us
  Pallas kernels  51.7 us (96%)
  between operations  1.35 us (3%)
    pallas_call x1, Pallas kernels, attention(): pl.pallas_call(functools.partial(kernel, ['q', 'k', 'v', 'g', 'lists'] +...  50.9 us

profile of v4, /device:TPU:0, one launch (start us, length us, event | category | flops | bytes accessed | tf_op | source)
XLA Modules:
  0.0 53.1 jit_solution(3202507877830152030)
XLA Ops:
  0.6 0.0 copy-start
  0.6 0.0 copy-start.1
  0.7 0.0 copy-start.2
  0.7 0.0 copy-start.3
  0.7 0.0 copy-start.4
  0.7 50.9 %block_sparse_attention.1 = (bf16[256,128]{1,0:T(8,128)(2,1)S(1)}, bf16[256,128]{1,0:T(8,128)(2,1)S(1)}, bf16[256,128]{1,0:T(8,128)(2,1)S(1)}, bf16[256,128]{1,0:T(8,128)(2,1)S(1)}, f32[1,1]{1,0:T(1,128)}) custom-call(bf16[2,128,128]{2,1,0:T(8,128)(2,1)} %bitcast.10, bf16[2,128,128]{2,1,0:T(8,128)(2,1)} %bitcast.12, bf16[2,128,128]{2,1,0:T(8,128)(2,1)} %bitcast.14, ...), custom_call_target="tpu_custom_call" | custom-call | tf_op jit(solution)/shard_map/block_sparse_attention/pallas_call | solution.py:601
  52.3 0.0 copy-done
  52.3 0.0 copy-done.1
  52.3 0.0 copy-done.2
  52.3 0.0 copy-done.3
  52.3 0.0 copy-done.4
  52.3 0.8 %conditional.1 = ((bf16[256,128]{1,0:T(8,128)(2,1)}, bf16[256,128]{1,0:T(8,128)(2,1)}, bf16[256,128]{1,0:T(8,128)(2,1)}, bf16[256,128]{1,0:T(8,128)(2,1)})) conditional(s32[]{:T(128)} %bitcast.9, (bf16[256,128]{1,0:T(8,128)(2,1)S(1)}, bf16[256,128]{1,0:T(8,128)(2,1)S(1)}, bf16[256,128]{1,0:T(8,128)(2,1)S(1)}, ...), branch_computations={%region_0.0_spmd, %region_1.0_spmd} | conditional | bytes 8 | solution.py:640
  52.3 0.7 %hand_out.2 = (bf16[256,128]{1,0:T(8,128)(2,1)}, bf16[256,128]{1,0:T(8,128)(2,1)}, bf16[256,128]{1,0:T(8,128)(2,1)}, bf16[256,128]{1,0:T(8,128)(2,1)}) custom-call(bf16[256,128]{1,0:T(8,128)(2,1)S(1)} %get-tuple-element.18.refs_0_, bf16[256,128]{1,0:T(8,128)(2,1)S(1)} %get-tuple-element.19.refs_1_, bf16[256,128]{1,0:T(8,128)(2,1)S(1)} %get-tuple-element.20.refs_2_, ...), custom_call_target="tpu_custom_call" | custom-call | tf_op jit(solution)/shard_map/cond/branch_0_fun/hand_out/pallas_call | solution.py:626
Async XLA Ops:
  0.6 51.6 %copy-start = (bf16[256,128]{1,0:T(8,128)(2,1)S(1)}, bf16[256,128]{1,0:T(8,128)(2,1)}, u32[]{:S(2)}) copy-start(bf16[256,128]{1,0:T(8,128)(2,1)} %param.7) | copy-start | bytes 196612
  0.6 51.6 %copy-start.1 = (bf16[256,128]{1,0:T(8,128)(2,1)S(1)}, bf16[256,128]{1,0:T(8,128)(2,1)}, u32[]{:S(2)}) copy-start(bf16[256,128]{1,0:T(8,128)(2,1)} %param.8) | copy-start | bytes 196612
  0.7 51.6 %copy-start.2 = (bf16[256,128]{1,0:T(8,128)(2,1)S(1)}, bf16[256,128]{1,0:T(8,128)(2,1)}, u32[]{:S(2)}) copy-start(bf16[256,128]{1,0:T(8,128)(2,1)} %param.9) | copy-start | bytes 196612
  0.7 51.6 %copy-start.3 = (bf16[256,128]{1,0:T(8,128)(2,1)S(1)}, bf16[256,128]{1,0:T(8,128)(2,1)}, u32[]{:S(2)}) copy-start(bf16[256,128]{1,0:T(8,128)(2,1)} %param.10) | copy-start | bytes 196612
  0.7 51.6 %copy-start.4 = (s32[256,16]{0,1:T(8,128)S(1)}, s32[256,16]{0,1:T(8,128)}, u32[]{:S(2)}) copy-start(s32[256,16]{0,1:T(8,128)} %param.11) | copy-start | bytes 49156

commit v5 on v4

--- a/solution.py
+++ b/solution.py
@@ -9,8 +9,8 @@
 from jax.sharding import PartitionSpec as P
 
 BLOCK = 128
-SLOTS = 64
-UNROLL = 32
+SLOTS = 56
+UNROLL = 28
 MESH = pl.DeviceIdType.MESH
 
 masked_score = -1e30
@@ -33,7 +33,7 @@
     return jnp.dot(left, right, preferred_element_type=jnp.float32)
 
 
-KEY, QUERY, SAME_KEY, DIAGONAL, PERM, PERM_KEY, SAME_QUERY, KEY_END, QUERY_END = range(9)
+KEY, QUERY, SAME_KEY, DIAGONAL, PERM, PERM_KEY, PERM_QUERY, SAME_QUERY, KEY_END, QUERY_END = range(10)
 LISTED = 16
 
 STAT_STEPS = ((False, 1), (False, -1), (True, 0), (False, 2), (True, 1), (True, -1), (True, 2))
@@ -80,7 +80,7 @@
     keys = fiota((32, 128), 0)
     id_col = (iota((32, 128), 0) // 2) * 16 + 2 * j + iota((32, 128), 0) % 2
     zero = jnp.zeros((32, 128), jnp.float32)
-    rows = {n: zero for n in range(7)}
+    rows = {n: zero for n in range(8)}
     for q in range(16):
         at_key = by_key[:, q : q + 1] == lane
         at_query = by_query[:, q : q + 1] == lane
@@ -90,9 +90,11 @@
         rows[DIAGONAL] += jnp.where(at_key & (id_col == query_id(i, j, q)), 1.0, 0.0)
         rows[PERM] += jnp.where(at_query, by_key[:, q : q + 1], 0.0)
         rows[PERM_KEY] += jnp.where(at_query, keys, 0.0)
+        rows[PERM_QUERY] += jnp.where(at_query, float(q), 0.0)
         rows[SAME_QUERY] += jnp.where(at_query, ones_where(in_query[:, q : q + 1] > 0), 0.0)
-    most = {KEY: 31, QUERY: 15, SAME_KEY: 1, DIAGONAL: 1, PERM: SLOTS - 1, PERM_KEY: 31, SAME_QUERY: 1}
-    for n in range(7):
+    most = {KEY: 31, QUERY: 15, SAME_KEY: 1, DIAGONAL: 1}
+    most |= {PERM: SLOTS - 1, PERM_KEY: 31, PERM_QUERY: 15, SAME_QUERY: 1}
+    for n in range(8):
         rows[n] = jnp.sum(rows[n], axis=0, keepdims=True)
         table[n : n + 1, :] = jnp.clip(rows[n].astype(jnp.int32), 0, most[n])
     key_end = jnp.where(key_count > 0, key_first + key_count, 0.0)
@@ -143,7 +145,7 @@
         self.blocks, self.gather_sems = blocks, gather_sems
         self.out, self.own_in, self.part_in, self.part_out = out, own_in, part_in, part_out
         self.sum_out, self.sum_in, self.sum_sems = sum_out, sum_in, sum_sems
-        self.copies = []
+        self.copies, self.waited = [], 0
 
     def at(self, step):
         return (self.p + step + 4) % 4
@@ -271,18 +273,18 @@
 
     loads = []
     for n, (src, dst) in enumerate(
-        ((r.k, kv.at[i, 0]), (r.v, kv.at[i, 1]), (r.q, qg.at[j, 0]), (r.g, qg.at[j, 1]))
+        ((r.k, kv.at[i, 0]), (r.q, qg.at[j, 0]), (r.v, kv.at[i, 1]), (r.g, qg.at[j, 1]), (r.lists, r.lists_v))
     ):
         loads.append(pltpu.make_async_copy(src, dst, r.local_sem.at[n]))
         loads[-1].start()
 
     stat_peers = [query_peer(pair, step) for pair, step in STAT_STEPS]
-    peers = [sibling, key_peer(True, 0), key_peer(False, 1), key_peer(False, -1)] + stat_peers
+    peers = [sibling, key_peer(True, 0), key_peer(False, 1), key_peer(False, -1)] + stat_peers[:3]
     barrier = pltpu.get_barrier_semaphore()
     for peer in peers:
         pl.semaphore_signal(barrier, inc=1, device_id=peer, device_id_type=MESH)
     pl.semaphore_wait(barrier, len(peers))
-    for load in loads:
+    for load in loads[:4]:
         load.wait()
 
     keys = Ring(
@@ -309,8 +311,9 @@
     to_sibling(i, 0)
     to_sibling(i, 1)
 
-    list_pairs(i, j, r.lists, r.table_v, None if dense else r.slot_query)
-    to_smem = pltpu.make_async_copy(r.table_v, table, r.local_sem.at[4])
+    loads[4].wait()
+    list_pairs(i, j, r.lists_v, r.table_v, None if dense else r.slot_query)
+    to_smem = pltpu.make_async_copy(r.table_v, table, r.local_sem.at[5])
     to_smem.start()
     gather_steps(0, 2, 4, 1, 3, 5)
 
@@ -322,7 +325,7 @@
     r.key_acc[none] = jnp.zeros(r.key_acc[none].shape, jnp.float32)
     r.query_acc[none] = jnp.zeros(r.query_acc[none].shape, jnp.float32)
     if not dense:
-        r.flag[0, 0] = most_pairs(r.lists)
+        r.flag[0, 0] = most_pairs(r.lists_v)
 
     gather_steps(8, 10, 9, 11, 6, 7, 12, 13)
     for copy in sib:
@@ -336,6 +339,12 @@
     r.stats[j] = r.stats_out[...]
     for n, peer in enumerate(stat_peers):
         st_copies.append(queries.send(r.stats_out, r.stats.at[j], st_sems, n, peer))
+    for ring in (keys, queries):
+        for copy in ring.copies[: -len(st_copies) if ring is queries else None]:
+            copy.wait_send()
+            ring.waited += 1
+    if not dense:
+        slot_query_grads(r)
     for copy in st_copies:
         copy.wait_recv()
     logs = r.stats[:, 0]
@@ -345,14 +354,22 @@
     for q in range(16):
         r.offsets[q] = offset[q : q + 1, :]
         r.deltas[q] = delta[q : q + 1, :]
+    if not dense:
+        scales = jnp.exp2(r.stats_out[0] - offset)
+        r.columns[...] = jnp.transpose(jnp.concatenate([scales, delta - r.stats_out[1]], axis=0))
 
     (dense_key_grads if dense else slot_key_grads)(r, i, j, scale)
 
     def key_part(block):
         return r.key_acc[block if dense else table[KEY_END, block]]
 
-    def query_part(block):
-        return r.query_acc[block if dense else table[QUERY_END, block]]
+    def query_part(q):
+        if dense:
+            return r.query_acc[q]
+        sums = r.query_acc[table[QUERY_END, q]]
+        own = r.columns[:, q : q + 1]
+        shift = r.columns[:, 16 + q : 17 + q]
+        return jnp.stack([own * (sums[0] - shift * sums[1]), own * sums[2]])
 
     swaps = []
     for phase, at in ((0, flip(x)), (1, x)):
@@ -380,49 +397,50 @@
 
         lax.fori_loop(0, 4, step, 0)
 
-    def query_out(at):
-        def step(n, carry):
+    def query_out(phase):
+        for n in range(4):
             for b in range(2):
-                r.query_out[at, n, :, b] = query_part((n * 2 + at) * 2 + b).astype(jnp.bfloat16)
-            return carry
-
-        lax.fori_loop(0, 4, step, 0)
-
-    if not dense:
-        slot_query_grads(r, 0, SLOTS // 2)
+                for at in range(2):
+
+                    @pl.when(at == (flip(h) if phase == 0 else h))
+                    def _(n=n, b=b, at=at):
+                        r.query_out[at, n, :, b] = query_part((n * 2 + at) * 2 + b).astype(jnp.bfloat16)
+
+    query_out(0)
+    query_sums = [queries.start_part(0)]
+    queries.start_plain(query_sums[0])
     key_out(0, flip(x))
     key_sums = [keys.start_part(0)]
     keys.start_plain(key_sums[0])
+    query_out(1)
+    query_sums.append(queries.start_part(1))
     key_out(1, x)
     key_sums.append(keys.start_part(1))
-    if not dense:
-        slot_query_grads(r, SLOTS // 2, SLOTS)
-    query_out(flip(h))
-    query_sums = [queries.start_part(0)]
-    queries.start_plain(query_sums[0])
+    queries.add_part(query_sums[0])
+    queries.start_plain(query_sums[1])
     keys.add_part(key_sums[0])
     keys.start_plain(key_sums[1])
-    query_out(h)
-    query_sums.append(queries.start_part(1))
-    queries.add_part(query_sums[0])
-    queries.start_plain(query_sums[1])
+    queries.add_part(query_sums[1])
     keys.add_part(key_sums[1])
+    queries.send_total(queries.total(query_sums[0]))
     keys.send_total(keys.total(key_sums[0]))
-    queries.add_part(query_sums[1])
-    queries.send_total(queries.total(query_sums[0]))
-    key_total = keys.total(key_sums[1]) + keys.other_total()
-    for b in range(2):
-        rows = pl.ds(b * BLOCK, BLOCK)
-        r.key_grads[rows, :] = (key_total[0, b] * scale).astype(jnp.bfloat16)
-        r.value_grads[rows, :] = key_total[1, b].astype(jnp.bfloat16)
-    query_total = queries.total(query_sums[1]) + queries.other_total()
-    for b in range(2):
-        rows = pl.ds(b * BLOCK, BLOCK)
-        r.query_grads[rows, :] = (query_total[0, b] * scale).astype(jnp.bfloat16)
-        r.attended[rows, :] = query_total[1, b].astype(jnp.bfloat16)
-
-    for copy in keys.copies + queries.copies:
-        copy.wait_send()
+    results = []
+
+    def finish(n, sums, factors, outs):
+        for m in range(2):
+            for b in range(2):
+                rows = pl.ds(b * BLOCK, BLOCK)
+                r.finals[n + m, rows, :] = (sums[m, b] * factors[m]).astype(jnp.bfloat16)
+            results.append(pltpu.make_async_copy(r.finals.at[n + m], outs[m], r.local_sem.at[6 + n + m]))
+            results[-1].start()
+
+    finish(0, queries.total(query_sums[1]) + queries.other_total(), (scale, 1.0), (r.query_grads, r.attended))
+    finish(2, keys.total(key_sums[1]) + keys.other_total(), (scale, 1.0), (r.key_grads, r.value_grads))
+    for ring in (keys, queries):
+        for copy in ring.copies[ring.waited :]:
+            copy.wait_send()
+    for result in results:
+        result.wait()
 
 
 def slot_stats(r, i, j, scale):
@@ -459,8 +477,11 @@
 def put_stats(r, q, top, total, moment):
     some = total > 0
     safe = jnp.where(some, total, 1.0)
-    r.stats_out[0, pl.ds(q, 1), :] = jnp.where(some, top + jnp.log2(safe), masked_score)
-    r.stats_out[1, pl.ds(q, 1), :] = moment / safe
+    log, mean = jnp.where(some, top + jnp.log2(safe), masked_score), moment / safe
+    r.stats_out[0, pl.ds(q, 1), :] = log
+    r.stats_out[1, pl.ds(q, 1), :] = mean
+    r.own_logs[q] = log
+    r.own_means[q] = mean
 
 
 def slot_key_grads(r, i, j, scale):
@@ -472,8 +493,6 @@
             prob = r.probs[s] * jnp.exp2(r.tops[pl.ds(s, 1), :] - r.offsets[q])
             weights = prob.astype(jnp.bfloat16)
             score_grad = (prob * (r.prob_grads[s] - r.deltas[q])).astype(jnp.bfloat16)
-            r.rounded[s, 0] = score_grad
-            r.rounded[s, 1] = weights
             r.key_acc[s + 1, 0] = r.key_acc[s, 0] * keep + dot(score_grad, r.qg[q // 2, 0, q % 2])
             r.key_acc[s + 1, 1] = r.key_acc[s, 1] * keep + dot(weights, r.qg[q // 2, 1, q % 2])
         return carry
@@ -481,18 +500,22 @@
     lax.fori_loop(0, SLOTS // UNROLL, step, 0)
 
 
-def slot_query_grads(r, first, last):
+def slot_query_grads(r):
     def step(n, carry):
         for u in range(UNROLL):
-            s = first + n * UNROLL + u
-            k, at = r.table[PERM_KEY, s], r.table[PERM, s]
+            s = n * UNROLL + u
+            k, q, at = r.table[PERM_KEY, s], r.table[PERM_QUERY, s], r.table[PERM, s]
             keep = r.table[SAME_QUERY, s].astype(jnp.float32)
-            for m in range(2):
-                new = across(r.rounded[at, m], r.kv[k // 2, m, k % 2])
-                r.query_acc[s + 1, m] = r.query_acc[s, m] * keep + new
+            prob = r.probs[at] * jnp.exp2(r.tops[pl.ds(at, 1), :] - r.own_logs[q])
+            weights = prob.astype(jnp.bfloat16)
+            score_grad = (prob * (r.prob_grads[at] - r.own_means[q])).astype(jnp.bfloat16)
+            keys, values = r.kv[k // 2, 0, k % 2], r.kv[k // 2, 1, k % 2]
+            r.query_acc[s + 1, 0] = r.query_acc[s, 0] * keep + across(score_grad, keys)
+            r.query_acc[s + 1, 1] = r.query_acc[s, 1] * keep + across(weights, keys)
+            r.query_acc[s + 1, 2] = r.query_acc[s, 2] * keep + across(weights, values)
         return carry
 
-    lax.fori_loop(0, (last - first) // UNROLL, step, 0)
+    lax.fori_loop(0, SLOTS // UNROLL, step, 0)
 
 
 def dense_tile(r, i, j, scale, q, k):
@@ -546,7 +569,6 @@
     table_rows = LISTED + 32 if dense else LISTED
     dma = pltpu.SemaphoreType.DMA
     any_spec = pl.BlockSpec(memory_space=pl.ANY)
-    vmem_spec = pl.BlockSpec(memory_space=pltpu.VMEM)
     smem_spec = pl.BlockSpec(memory_space=pltpu.SMEM)
     scratch = {
         "kv": pltpu.VMEM((16, 2, 2) + tile, bf16),
@@ -559,10 +581,14 @@
         "offsets": pltpu.VMEM((16, 1, 128), f32),
         "deltas": pltpu.VMEM((16, 1, 128), f32),
         "key_acc": pltpu.VMEM((32 if dense else SLOTS + 1, 2) + tile, f32),
-        "query_acc": pltpu.VMEM((16 if dense else SLOTS + 1, 2) + tile, f32),
+        "query_acc": pltpu.VMEM(((16, 2) if dense else (SLOTS + 1, 3)) + tile, f32),
+        "own_logs": pltpu.VMEM((16, 1, 128), f32),
+        "own_means": pltpu.VMEM((16, 1, 128), f32),
         "sib_out": pltpu.VMEM((2, 4, 2, 2) + tile, bf16),
         "sib_in": pltpu.VMEM((2, 4, 2, 2) + tile, bf16),
-        "local_sem": dma((5,)),
+        "lists_v": pltpu.VMEM((16, 256), jnp.int32),
+        "finals": pltpu.VMEM((4, 2 * BLOCK, BLOCK), bf16),
+        "local_sem": dma((10,)),
         "kv_send": dma((14,)),
         "kv_recv": dma((14,)),
         "qg_send": dma((14,)),
@@ -591,17 +617,17 @@
             "tops": pltpu.VMEM((SLOTS, 128), f32),
             "totals": pltpu.VMEM((SLOTS, 128), f32),
             "moments": pltpu.VMEM((SLOTS, 128), f32),
-            "rounded": pltpu.VMEM((SLOTS, 2) + tile, bf16),
+            "columns": pltpu.VMEM((BLOCK, 32), f32),
         }
     outs = ["attended", "query_grads", "key_grads", "value_grads"] + ["flag"] * (not dense)
-    out_shape, out_specs = [out] * 4, [vmem_spec] * 4
+    out_shape, out_specs = [out] * 4, [any_spec] * 4
     if not dense:
         out_shape.append(jax.ShapeDtypeStruct((1, 1), f32))
         out_specs.append(smem_spec)
     return pl.pallas_call(
         functools.partial(kernel, ["q", "k", "v", "g", "lists"] + outs + list(scratch), dense),
         out_shape=out_shape,
-        in_specs=[any_spec] * 4 + [vmem_spec],
+        in_specs=[any_spec] * 5,
         out_specs=out_specs,
         scratch_shapes=list(scratch.values()),
         compiler_params=pltpu.CompilerParams(

time: 53.7 us -> 49.6 us (0.924)
  Pallas kernels: 51.7 us -> 47.7 us
    pallas_call x1, Pallas kernels: 50.9 us -> 47 us  [attention(): pl.pallas_call(functools.partial(kernel, ['q', 'k', 'v', 'g', 'lists'] +...]
where the time goes in v5:
time: 49.6 us; the launch traced here: 49.1 us
  Pallas kernels  47.7 us (96%)
  between operations  1.35 us (3%)
    pallas_call x1, Pallas kernels, attention(): pl.pallas_call(functools.partial(kernel, ['q', 'k', 'v', 'g', 'lists'] +...  47 us

profile of v5, /device:TPU:0, one launch (start us, length us, event | category | flops | bytes accessed | tf_op | source)
XLA Modules:
  0.0 49.1 jit_solution(6798426151971781180)
XLA Ops:
  0.6 0.0 copy-start
  0.6 0.0 copy-start.1
  0.7 0.0 copy-start.2
  0.7 0.0 copy-start.3
  0.7 0.0 copy-start.4
  0.7 47.0 %block_sparse_attention.1 = (bf16[256,128]{1,0:T(8,128)(2,1)S(1)}, bf16[256,128]{1,0:T(8,128)(2,1)S(1)}, bf16[256,128]{1,0:T(8,128)(2,1)S(1)}, bf16[256,128]{1,0:T(8,128)(2,1)S(1)}, f32[1,1]{1,0:T(1,128)}) custom-call(bf16[2,128,128]{2,1,0:T(8,128)(2,1)} %bitcast.10, bf16[2,128,128]{2,1,0:T(8,128)(2,1)} %bitcast.12, bf16[2,128,128]{2,1,0:T(8,128)(2,1)} %bitcast.14, ...), custom_call_target="tpu_custom_call" | custom-call | tf_op jit(solution)/shard_map/block_sparse_attention/pallas_call | solution.py:627
  48.3 0.0 copy-done
  48.3 0.0 copy-done.1
  48.3 0.0 copy-done.2
  48.3 0.0 copy-done.3
  48.3 0.0 copy-done.4
  48.3 0.8 %conditional.1 = ((bf16[256,128]{1,0:T(8,128)(2,1)}, bf16[256,128]{1,0:T(8,128)(2,1)}, bf16[256,128]{1,0:T(8,128)(2,1)}, bf16[256,128]{1,0:T(8,128)(2,1)})) conditional(s32[]{:T(128)} %bitcast.9, (bf16[256,128]{1,0:T(8,128)(2,1)S(1)}, bf16[256,128]{1,0:T(8,128)(2,1)S(1)}, bf16[256,128]{1,0:T(8,128)(2,1)S(1)}, ...), branch_computations={%region_0.0_spmd, %region_1.0_spmd} | conditional | bytes 8 | solution.py:666
  48.3 0.7 %hand_out.2 = (bf16[256,128]{1,0:T(8,128)(2,1)}, bf16[256,128]{1,0:T(8,128)(2,1)}, bf16[256,128]{1,0:T(8,128)(2,1)}, bf16[256,128]{1,0:T(8,128)(2,1)}) custom-call(bf16[256,128]{1,0:T(8,128)(2,1)S(1)} %get-tuple-element.18.refs_0_, bf16[256,128]{1,0:T(8,128)(2,1)S(1)} %get-tuple-element.19.refs_1_, bf16[256,128]{1,0:T(8,128)(2,1)S(1)} %get-tuple-element.20.refs_2_, ...), custom_call_target="tpu_custom_call" | custom-call | tf_op jit(solution)/shard_map/cond/branch_0_fun/hand_out/pallas_call | solution.py:652
Async XLA Ops:
  0.6 47.6 %copy-start = (bf16[256,128]{1,0:T(8,128)(2,1)S(1)}, bf16[256,128]{1,0:T(8,128)(2,1)}, u32[]{:S(2)}) copy-start(bf16[256,128]{1,0:T(8,128)(2,1)} %param.7) | copy-start | bytes 196612
  0.6 47.6 %copy-start.1 = (bf16[256,128]{1,0:T(8,128)(2,1)S(1)}, bf16[256,128]{1,0:T(8,128)(2,1)}, u32[]{:S(2)}) copy-start(bf16[256,128]{1,0:T(8,128)(2,1)} %param.8) | copy-start | bytes 196612
  0.7 47.6 %copy-start.2 = (bf16[256,128]{1,0:T(8,128)(2,1)S(1)}, bf16[256,128]{1,0:T(8,128)(2,1)}, u32[]{:S(2)}) copy-start(bf16[256,128]{1,0:T(8,128)(2,1)} %param.9) | copy-start | bytes 196612
  0.7 47.6 %copy-start.3 = (bf16[256,128]{1,0:T(8,128)(2,1)S(1)}, bf16[256,128]{1,0:T(8,128)(2,1)}, u32[]{:S(2)}) copy-start(bf16[256,128]{1,0:T(8,128)(2,1)} %param.10) | copy-start | bytes 196612
  0.7 47.6 %copy-start.4 = (s32[256,16]{0,1:T(8,128)S(1)}, s32[256,16]{0,1:T(8,128)}, u32[]{:S(2)}) copy-start(s32[256,16]{0,1:T(8,128)} %param.11) | copy-start | bytes 49156

commit v6 on v5

--- a/solution.py
+++ b/solution.py
@@ -130,11 +130,6 @@
     return jnp.max(dot(counts, member))
 
 
-class Refs:
-    def __init__(self, names, refs):
-        self.__dict__.update(zip(names, refs, strict=True))
-
-
 def flip(bit):
     return 1 - bit
 
@@ -165,9 +160,11 @@
 
     def start_own(self):
         own, up, down = self.row(self.a, self.p), self.peer(False, 1), self.peer(False, -1)
-        self.gather = {0: self.pass_half(0, own, 0, self.peer(True, 0))}
-        self.gather[2] = self.pass_half(2, own, 0, up)
+        self.gather = {2: self.pass_half(2, own, 0, up)}
         self.gather[4] = self.pass_half(4, own, 1, down)
+        self.gather[8] = self.pass_half(8, own, 0, self.peer(True, 1))
+        self.gather[10] = self.pass_half(10, own, 1, self.peer(True, -1))
+        self.gather[0] = self.pass_half(0, own, 0, self.peer(True, 0))
         self.gather[1] = self.pass_half(1, own, 1, self.peer(True, 0))
         self.gather[3] = self.pass_half(3, own, 1, up)
         self.gather[5] = self.pass_half(5, own, 0, down)
@@ -178,11 +175,9 @@
         if n < 2:
             row = self.row(flip(self.a), self.p)
             if n == 0:
-                self.gather[8] = self.pass_half(8, row, 0, up)
+                self.gather[11] = self.pass_half(11, row, 0, down)
             else:
-                self.gather[10] = self.pass_half(10, row, 1, down)
                 self.gather[9] = self.pass_half(9, row, 1, up)
-                self.gather[11] = self.pass_half(11, row, 0, down)
             return row, n
         a = self.a if n < 8 else flip(self.a)
         m = (n - 2) % 6
@@ -194,53 +189,73 @@
             self.gather[n + 3] = self.pass_half(n + 3, row, half, down)
         return row, half
 
-    def start_part(self, phase):
+    def pieces(self, phase):
+        return [(half, b) for b in ((0, 1) if phase == 0 else (None,)) for half in (0, 1)]
+
+    def start_part(self, phase, cross=None):
         a = flip(self.a) if phase == 0 else self.a
-        out, sems, n = self.out, self.sum_sems, 6 * phase
-        opposite = self.at(2)
-        part = [
-            self.send(out.at[a, opposite, 0], self.part_in.at[phase, 0], sems, n, self.peer(False, 1)),
-            self.send(out.at[a, opposite, 1], self.part_in.at[phase, 1], sems, n + 1, self.peer(False, -1)),
+        parts = {}
+        for half, b in self.pieces(phase):
+            n = 12 + half if b is None else 2 * half + b
+            step = 1 if half == 0 else -1
+            src, dst = self.out.at[a, self.at(2), half], self.part_in.at[phase, half]
+            if b is not None:
+                src, dst = src.at[b], dst.at[b]
+            parts[half, b] = [self.send(src, dst, self.sum_sems, n, self.peer(False, step))]
+            if cross is not None:
+                cross_out, cross_in, cross_peer = cross
+                parts[half, b].append(
+                    self.send(
+                        cross_out.at[half, b], cross_in.at[half, b], self.sum_sems, 18 + n, cross_peer(step)
+                    )
+                )
+        return [a, phase, parts, [], {}, cross]
+
+    def start_plain(self, state):
+        a, phase, _, plain, _, _ = state
+        out, sems, n = self.out, self.sum_sems, 4 + 10 * phase
+        plain += [
+            self.send(out.at[a, self.at(1), 1], self.own_in.at[phase, 1], sems, n, self.peer(False, 1)),
+            self.send(out.at[a, self.at(-1), 0], self.own_in.at[phase, 0], sems, n + 1, self.peer(False, -1)),
         ]
-        return [a, phase, part, [], []]
-
-    def start_plain(self, state):
-        a, phase, _, plain, _ = state
-        out, sems, n = self.out, self.sum_sems, 6 * phase
-        plain += [
-            self.send(out.at[a, self.at(1), 1], self.own_in.at[phase, 1], sems, n + 2, self.peer(False, 1)),
-            self.send(out.at[a, self.at(-1), 0], self.own_in.at[phase, 0], sems, n + 3, self.peer(False, -1)),
-        ]
 
     def add_part(self, state):
-        a, phase, part, _, summed = state
-        n = 6 * phase + 4
-        for half, step in ((0, 1), (1, -1)):
-            part[half].wait_recv()
-            both = self.out[a, self.at(step), half].astype(jnp.float32) + self.part_in[phase, half].astype(jnp.float32)
-            self.part_out[phase, half] = both.astype(jnp.bfloat16)
-            summed.append(
-                self.send(
-                    self.part_out.at[phase, half], self.own_in.at[phase, 2 + half], self.sum_sems, n + half,
-                    self.peer(False, step),
-                )
-            )
-
-    def total(self, state):
-        a, phase, _, plain, summed = state
-        for copy in plain + summed:
-            copy.wait_recv()
-        total = self.out[a, self.p].astype(jnp.float32)
-        total += self.own_in[phase, 0:2].astype(jnp.float32)
-        return total + self.own_in[phase, 2:4].astype(jnp.float32)
-
-    def send_total(self, total):
-        self.sum_out[...] = total.astype(jnp.bfloat16)
-        self.across_pair = self.send(self.sum_out, self.sum_in, self.sum_sems, 12, self.peer(True, 0))
-
-    def other_total(self):
-        self.across_pair.wait_recv()
-        return self.sum_in[...].astype(jnp.float32)
+        a, phase, parts, _, sums, cross = state
+        for half, b in self.pieces(phase):
+            n = 16 + half if b is None else 6 + 2 * half + b
+            step = 1 if half == 0 else -1
+            for copy in parts[half, b]:
+                copy.wait_recv()
+            at = slice(None) if b is None else b
+            both = self.out[a, self.at(step), half, at].astype(jnp.float32)
+            both += self.part_in[phase, half, at].astype(jnp.float32)
+            if cross is not None:
+                both += cross[1][half, at].astype(jnp.float32)
+            self.part_out[phase, half, at] = both.astype(jnp.bfloat16)
+            src, dst = self.part_out.at[phase, half], self.own_in.at[phase, 2 + half]
+            if b is not None:
+                src, dst = src.at[b], dst.at[b]
+            sums[half, b] = self.send(src, dst, self.sum_sems, n, self.peer(False, step))
+
+    def total(self, state, b):
+        a, phase, _, plain, sums, _ = state
+        while plain:
+            plain.pop().wait_recv()
+        for piece in [piece for piece in sums if piece[1] in (b, None)]:
+            sums.pop(piece).wait_recv()
+        total = self.out[a, self.p, :, b].astype(jnp.float32)
+        total += self.own_in[phase, 0:2, b].astype(jnp.float32)
+        return total + self.own_in[phase, 2:4, b].astype(jnp.float32)
+
+    def send_total(self, state, b):
+        self.sum_out[b] = self.total(state, b).astype(jnp.bfloat16)
+        copy = self.send(self.sum_out.at[b], self.sum_in.at[b], self.sum_sems, 10 + b, self.peer(True, 0))
+        self.to_total = getattr(self, "to_total", {}) | {b: copy}
+
+    def whole_total(self, state, b):
+        total = self.total(state, b)
+        self.to_total[b].wait_recv()
+        return total + self.sum_in[b].astype(jnp.float32)
 
 
 class Refs:
@@ -279,7 +294,7 @@
         loads[-1].start()
 
     stat_peers = [query_peer(pair, step) for pair, step in STAT_STEPS]
-    peers = [sibling, key_peer(True, 0), key_peer(False, 1), key_peer(False, -1)] + stat_peers[:3]
+    peers = [sibling, key_peer(True, 0), key_peer(False, 1), key_peer(False, -1), key_peer(True, 1), key_peer(True, -1)] + stat_peers[:3] + stat_peers[4:6]
     barrier = pltpu.get_barrier_semaphore()
     for peer in peers:
         pl.semaphore_signal(barrier, inc=1, device_id=peer, device_id_type=MESH)
@@ -315,7 +330,7 @@
     list_pairs(i, j, r.lists_v, r.table_v, None if dense else r.slot_query)
     to_smem = pltpu.make_async_copy(r.table_v, table, r.local_sem.at[5])
     to_smem.start()
-    gather_steps(0, 2, 4, 1, 3, 5)
+    gather_steps(2, 4, 0, 1, 8, 10)
 
     r.bias[0] = jnp.zeros((BLOCK, BLOCK), jnp.float32)
     r.bias[1] = jnp.where(
@@ -327,7 +342,7 @@
     if not dense:
         r.flag[0, 0] = most_pairs(r.lists_v)
 
-    gather_steps(8, 10, 9, 11, 6, 7, 12, 13)
+    gather_steps(3, 5, 6, 7, 9, 11, 12, 13)
     for copy in sib:
         copy.wait_recv()
     to_smem.wait()
@@ -358,11 +373,8 @@
         scales = jnp.exp2(r.stats_out[0] - offset)
         r.columns[...] = jnp.transpose(jnp.concatenate([scales, delta - r.stats_out[1]], axis=0))
 
-    (dense_key_grads if dense else slot_key_grads)(r, i, j, scale)
-
-    def key_part(block):
-        return r.key_acc[block if dense else table[KEY_END, block]]
-
+    if dense:
+        dense_key_grads(r, i, j, scale)
     def query_part(q):
         if dense:
             return r.query_acc[q]
@@ -371,32 +383,6 @@
         shift = r.columns[:, 16 + q : 17 + q]
         return jnp.stack([own * (sums[0] - shift * sums[1]), own * sums[2]])
 
-    swaps = []
-    for phase, at in ((0, flip(x)), (1, x)):
-
-        def sib_step(n, carry, phase=phase, at=at):
-            owner = at * 8 + n * 2 + 1 - core
-            for b in range(2):
-                r.sib_out[phase, n, :, b] = key_part(owner * 2 + b).astype(jnp.bfloat16)
-            return carry
-
-        lax.fori_loop(0, 4, sib_step, 0)
-        swaps.append(
-            keys.send(r.sib_out.at[phase], r.sib_in.at[phase], (r.sib_send, r.sib_recv), 16 + phase, sibling)
-        )
-
-    def key_out(phase, at):
-        swaps[phase].wait_recv()
-
-        def step(n, carry):
-            owner = at * 8 + n * 2 + core
-            for b in range(2):
-                both = key_part(owner * 2 + b) + r.sib_in[phase, n, :, b].astype(jnp.float32)
-                r.key_out[at, n, :, b] = both.astype(jnp.bfloat16)
-            return carry
-
-        lax.fori_loop(0, 4, step, 0)
-
     def query_out(phase):
         for n in range(4):
             for b in range(2):
@@ -409,33 +395,78 @@
     query_out(0)
     query_sums = [queries.start_part(0)]
     queries.start_plain(query_sums[0])
-    key_out(0, flip(x))
-    key_sums = [keys.start_part(0)]
-    keys.start_plain(key_sums[0])
+    if not dense:
+        slot_key_grads(r, i, j, scale)
+
+    def key_part(block):
+        return r.key_acc[block if dense else table[KEY_END, block]]
+
+    def key_owner(at, step, parity):
+        return at * 8 + keys.at(step) * 2 + parity
+
+    for b in range(2):
+        same = key_part(key_owner(flip(x), 2, core) * 2 + b).astype(jnp.bfloat16)
+        other = key_part(key_owner(flip(x), 2, 1 - core) * 2 + b).astype(jnp.bfloat16)
+        for half in range(2):
+            r.key_out[flip(x), keys.at(2), half, b] = same[half]
+            r.cross_out[half, b] = other[half]
+
+    def cross_peer(step):
+        return (x * 8 + keys.at(step) * 2 + 1 - core, j)
+
+    key_sums = [keys.start_part(0, (r.cross_out, r.cross_in, cross_peer))]
+
+    swaps = []
+    ring_steps = ((0, 1, -1), (0, 1, -1, 2))
+    for phase, at in ((0, flip(x)), (1, x)):
+        for n, step in enumerate(ring_steps[phase]):
+            for b in range(2):
+                block = key_owner(at, step, 1 - core) * 2 + b
+                r.sib_out[phase, n, :, b] = key_part(block).astype(jnp.bfloat16)
+        some = pl.ds(0, len(ring_steps[phase]))
+        swaps.append(
+            keys.send(
+                r.sib_out.at[phase, some], r.sib_in.at[phase, some], (r.sib_send, r.sib_recv), 16 + phase, sibling
+            )
+        )
+
+    def key_out(phase, at):
+        swaps[phase].wait_recv()
+        for n, step in enumerate(ring_steps[phase]):
+            for b in range(2):
+                both = key_part(key_owner(at, step, core) * 2 + b) + r.sib_in[phase, n, :, b].astype(jnp.float32)
+                r.key_out[at, keys.at(step), :, b] = both.astype(jnp.bfloat16)
+
     query_out(1)
     query_sums.append(queries.start_part(1))
+    queries.add_part(query_sums[0])
+    queries.start_plain(query_sums[1])
+    key_out(0, flip(x))
+    keys.start_plain(key_sums[0])
+    keys.add_part(key_sums[0])
     key_out(1, x)
     key_sums.append(keys.start_part(1))
-    queries.add_part(query_sums[0])
-    queries.start_plain(query_sums[1])
-    keys.add_part(key_sums[0])
     keys.start_plain(key_sums[1])
+    for b in range(2):
+        queries.send_total(query_sums[0], b)
     queries.add_part(query_sums[1])
+    for b in range(2):
+        keys.send_total(key_sums[0], b)
     keys.add_part(key_sums[1])
-    queries.send_total(queries.total(query_sums[0]))
-    keys.send_total(keys.total(key_sums[0]))
     results = []
 
-    def finish(n, sums, factors, outs):
+    def finish(n, ring, state, factors, outs):
+        for b in range(2):
+            rows = pl.ds(b * BLOCK, BLOCK)
+            sums = ring.whole_total(state, b)
+            for m in range(2):
+                r.finals[n + m, rows, :] = (sums[m] * factors[m]).astype(jnp.bfloat16)
         for m in range(2):
-            for b in range(2):
-                rows = pl.ds(b * BLOCK, BLOCK)
-                r.finals[n + m, rows, :] = (sums[m, b] * factors[m]).astype(jnp.bfloat16)
             results.append(pltpu.make_async_copy(r.finals.at[n + m], outs[m], r.local_sem.at[6 + n + m]))
             results[-1].start()
 
-    finish(0, queries.total(query_sums[1]) + queries.other_total(), (scale, 1.0), (r.query_grads, r.attended))
-    finish(2, keys.total(key_sums[1]) + keys.other_total(), (scale, 1.0), (r.key_grads, r.value_grads))
+    finish(0, queries, query_sums[1], (scale, 1.0), (r.query_grads, r.attended))
+    finish(2, keys, key_sums[1], (scale, 1.0), (r.key_grads, r.value_grads))
     for ring in (keys, queries):
         for copy in ring.copies[ring.waited :]:
             copy.wait_send()
@@ -584,6 +615,8 @@
         "query_acc": pltpu.VMEM(((16, 2) if dense else (SLOTS + 1, 3)) + tile, f32),
         "own_logs": pltpu.VMEM((16, 1, 128), f32),
         "own_means": pltpu.VMEM((16, 1, 128), f32),
+        "cross_out": pltpu.VMEM((2, 2) + tile, bf16),
+        "cross_in": pltpu.VMEM((2, 2) + tile, bf16),
         "sib_out": pltpu.VMEM((2, 4, 2, 2) + tile, bf16),
         "sib_in": pltpu.VMEM((2, 4, 2, 2) + tile, bf16),
         "lists_v": pltpu.VMEM((16, 256), jnp.int32),
@@ -606,8 +639,8 @@
             ring + "_part_out": pltpu.VMEM((2, 2, 2) + tile, bf16),
             ring + "_sum_out": pltpu.VMEM((2, 2) + tile, bf16),
             ring + "_sum_in": pltpu.VMEM((2, 2) + tile, bf16),
-            ring + "_send": dma((13,)),
-            ring + "_recv": dma((13,)),
+            ring + "_send": dma((22,)),
+            ring + "_recv": dma((22,)),
         }
     if not dense:
         scratch |= {

time: 49.6 us -> 48.9 us (0.986)
  no operation moved by 1% of the time
where the time goes in v6:
time: 48.9 us; the launch traced here: 48.8 us
  Pallas kernels  47.4 us (97%)
  between operations  1.35 us (3%)
    pallas_call x1, Pallas kernels, attention(): pl.pallas_call(functools.partial(kernel, ['q', 'k', 'v', 'g', 'lists'] +...  46.7 us

profile of v6, /device:TPU:0, one launch (start us, length us, event | category | flops | bytes accessed | tf_op | source)
XLA Modules:
  0.0 48.8 jit_solution(12768743503668490294)
XLA Ops:
  0.6 0.0 copy-start
  0.6 0.0 copy-start.1
  0.7 0.0 copy-start.2
  0.7 0.0 copy-start.3
  0.7 0.0 copy-start.4
  0.7 46.7 %block_sparse_attention.1 = (bf16[256,128]{1,0:T(8,128)(2,1)S(1)}, bf16[256,128]{1,0:T(8,128)(2,1)S(1)}, bf16[256,128]{1,0:T(8,128)(2,1)S(1)}, bf16[256,128]{1,0:T(8,128)(2,1)S(1)}, f32[1,1]{1,0:T(1,128)}) custom-call(bf16[2,128,128]{2,1,0:T(8,128)(2,1)} %bitcast.10, bf16[2,128,128]{2,1,0:T(8,128)(2,1)} %bitcast.12, bf16[2,128,128]{2,1,0:T(8,128)(2,1)} %bitcast.14, ...), custom_call_target="tpu_custom_call" | custom-call | tf_op jit(solution)/shard_map/block_sparse_attention/pallas_call | solution.py:660
  48.0 0.0 copy-done
  48.0 0.0 copy-done.1
  48.0 0.0 copy-done.2
  48.0 0.0 copy-done.3
  48.0 0.0 copy-done.4
  48.0 0.8 %conditional.1 = ((bf16[256,128]{1,0:T(8,128)(2,1)}, bf16[256,128]{1,0:T(8,128)(2,1)}, bf16[256,128]{1,0:T(8,128)(2,1)}, bf16[256,128]{1,0:T(8,128)(2,1)})) conditional(s32[]{:T(128)} %bitcast.9, (bf16[256,128]{1,0:T(8,128)(2,1)S(1)}, bf16[256,128]{1,0:T(8,128)(2,1)S(1)}, bf16[256,128]{1,0:T(8,128)(2,1)S(1)}, ...), branch_computations={%region_0.0_spmd, %region_1.0_spmd} | conditional | bytes 8 | solution.py:699
  48.0 0.7 %hand_out.2 = (bf16[256,128]{1,0:T(8,128)(2,1)}, bf16[256,128]{1,0:T(8,128)(2,1)}, bf16[256,128]{1,0:T(8,128)(2,1)}, bf16[256,128]{1,0:T(8,128)(2,1)}) custom-call(bf16[256,128]{1,0:T(8,128)(2,1)S(1)} %get-tuple-element.18.refs_0_, bf16[256,128]{1,0:T(8,128)(2,1)S(1)} %get-tuple-element.19.refs_1_, bf16[256,128]{1,0:T(8,128)(2,1)S(1)} %get-tuple-element.20.refs_2_, ...), custom_call_target="tpu_custom_call" | custom-call | tf_op jit(solution)/shard_map/cond/branch_0_fun/hand_out/pallas_call | solution.py:685
Async XLA Ops:
  0.6 47.4 %copy-start = (bf16[256,128]{1,0:T(8,128)(2,1)S(1)}, bf16[256,128]{1,0:T(8,128)(2,1)}, u32[]{:S(2)}) copy-start(bf16[256,128]{1,0:T(8,128)(2,1)} %param.7) | copy-start | bytes 196612
  0.6 47.4 %copy-start.1 = (bf16[256,128]{1,0:T(8,128)(2,1)S(1)}, bf16[256,128]{1,0:T(8,128)(2,1)}, u32[]{:S(2)}) copy-start(bf16[256,128]{1,0:T(8,128)(2,1)} %param.8) | copy-start | bytes 196612
  0.7 47.4 %copy-start.2 = (bf16[256,128]{1,0:T(8,128)(2,1)S(1)}, bf16[256,128]{1,0:T(8,128)(2,1)}, u32[]{:S(2)}) copy-start(bf16[256,128]{1,0:T(8,128)(2,1)} %param.9) | copy-start | bytes 196612
  0.7 47.4 %copy-start.3 = (bf16[256,128]{1,0:T(8,128)(2,1)S(1)}, bf16[256,128]{1,0:T(8,128)(2,1)}, u32[]{:S(2)}) copy-start(bf16[256,128]{1,0:T(8,128)(2,1)} %param.10) | copy-start | bytes 196612
  0.7 47.4 %copy-start.4 = (s32[256,16]{0,1:T(8,128)S(1)}, s32[256,16]{0,1:T(8,128)}, u32[]{:S(2)}) copy-start(s32[256,16]{0,1:T(8,128)} %param.11) | copy-start | bytes 49156

commit v7 on v6

--- a/solution.py
+++ b/solution.py
@@ -10,7 +10,7 @@
 
 BLOCK = 128
 SLOTS = 56
-UNROLL = 28
+UNROLL = 56
 MESH = pl.DeviceIdType.MESH
 
 masked_score = -1e30

time: 48.9 us -> 48.6 us (level)
  no operation moved by 1% of the time
where the time goes in v7:
time: 48.6 us; the launch traced here: 48.5 us
  Pallas kernels  47.1 us (97%)
  between operations  1.35 us (3%)
    pallas_call x1, Pallas kernels, attention(): pl.pallas_call(functools.partial(kernel, ['q', 'k', 'v', 'g', 'lists'] +...  46.3 us

profile of v7, /device:TPU:0, one launch (start us, length us, event | category | flops | bytes accessed | tf_op | source)
XLA Modules:
  0.0 48.5 jit_solution(9004769224110923791)
XLA Ops:
  0.6 0.0 copy-start
  0.6 0.0 copy-start.1
  0.7 0.0 copy-start.2
  0.7 0.0 copy-start.3
  0.7 0.0 copy-start.4
  0.7 46.3 %block_sparse_attention.1 = (bf16[256,128]{1,0:T(8,128)(2,1)S(1)}, bf16[256,128]{1,0:T(8,128)(2,1)S(1)}, bf16[256,128]{1,0:T(8,128)(2,1)S(1)}, bf16[256,128]{1,0:T(8,128)(2,1)S(1)}, f32[1,1]{1,0:T(1,128)}) custom-call(bf16[2,128,128]{2,1,0:T(8,128)(2,1)} %bitcast.10, bf16[2,128,128]{2,1,0:T(8,128)(2,1)} %bitcast.12, bf16[2,128,128]{2,1,0:T(8,128)(2,1)} %bitcast.14, ...), custom_call_target="tpu_custom_call" | custom-call | tf_op jit(solution)/shard_map/block_sparse_attention/pallas_call | solution.py:660
  47.7 0.0 copy-done
  47.7 0.0 copy-done.1
  47.7 0.0 copy-done.2
  47.7 0.0 copy-done.3
  47.7 0.0 copy-done.4
  47.7 0.8 %conditional.1 = ((bf16[256,128]{1,0:T(8,128)(2,1)}, bf16[256,128]{1,0:T(8,128)(2,1)}, bf16[256,128]{1,0:T(8,128)(2,1)}, bf16[256,128]{1,0:T(8,128)(2,1)})) conditional(s32[]{:T(128)} %bitcast.9, (bf16[256,128]{1,0:T(8,128)(2,1)S(1)}, bf16[256,128]{1,0:T(8,128)(2,1)S(1)}, bf16[256,128]{1,0:T(8,128)(2,1)S(1)}, ...), branch_computations={%region_0.0_spmd, %region_1.0_spmd} | conditional | bytes 8 | solution.py:699
  47.7 0.7 %hand_out.2 = (bf16[256,128]{1,0:T(8,128)(2,1)}, bf16[256,128]{1,0:T(8,128)(2,1)}, bf16[256,128]{1,0:T(8,128)(2,1)}, bf16[256,128]{1,0:T(8,128)(2,1)}) custom-call(bf16[256,128]{1,0:T(8,128)(2,1)S(1)} %get-tuple-element.18.refs_0_, bf16[256,128]{1,0:T(8,128)(2,1)S(1)} %get-tuple-element.19.refs_1_, bf16[256,128]{1,0:T(8,128)(2,1)S(1)} %get-tuple-element.20.refs_2_, ...), custom_call_target="tpu_custom_call" | custom-call | tf_op jit(solution)/shard_map/cond/branch_0_fun/hand_out/pallas_call | solution.py:685
Async XLA Ops:
  0.6 47.0 %copy-start = (bf16[256,128]{1,0:T(8,128)(2,1)S(1)}, bf16[256,128]{1,0:T(8,128)(2,1)}, u32[]{:S(2)}) copy-start(bf16[256,128]{1,0:T(8,128)(2,1)} %param.7) | copy-start | bytes 196612
  0.6 47.0 %copy-start.1 = (bf16[256,128]{1,0:T(8,128)(2,1)S(1)}, bf16[256,128]{1,0:T(8,128)(2,1)}, u32[]{:S(2)}) copy-start(bf16[256,128]{1,0:T(8,128)(2,1)} %param.8) | copy-start | bytes 196612
  0.7 47.0 %copy-start.2 = (bf16[256,128]{1,0:T(8,128)(2,1)S(1)}, bf16[256,128]{1,0:T(8,128)(2,1)}, u32[]{:S(2)}) copy-start(bf16[256,128]{1,0:T(8,128)(2,1)} %param.9) | copy-start | bytes 196612
  0.7 47.0 %copy-start.3 = (bf16[256,128]{1,0:T(8,128)(2,1)S(1)}, bf16[256,128]{1,0:T(8,128)(2,1)}, u32[]{:S(2)}) copy-start(bf16[256,128]{1,0:T(8,128)(2,1)} %param.10) | copy-start | bytes 196612
  0.7 47.0 %copy-start.4 = (s32[256,16]{0,1:T(8,128)S(1)}, s32[256,16]{0,1:T(8,128)}, u32[]{:S(2)}) copy-start(s32[256,16]{0,1:T(8,128)} %param.11) | copy-start | bytes 49156

commit v8 on v7

--- a/solution.py
+++ b/solution.py
@@ -339,8 +339,6 @@
     none = 0 if not dense else slice(None)
     r.key_acc[none] = jnp.zeros(r.key_acc[none].shape, jnp.float32)
     r.query_acc[none] = jnp.zeros(r.query_acc[none].shape, jnp.float32)
-    if not dense:
-        r.flag[0, 0] = most_pairs(r.lists_v)
 
     gather_steps(3, 5, 6, 7, 9, 11, 12, 13)
     for copy in sib:
@@ -359,6 +357,7 @@
             copy.wait_send()
             ring.waited += 1
     if not dense:
+        r.flag[0, 0] = most_pairs(r.lists_v)
         slot_query_grads(r)
     for copy in st_copies:
         copy.wait_recv()

time: 48.6 us -> 49 us (level)
  no operation moved by 1% of the time
where the time goes in v8:
time: 49 us; the launch traced here: 48.9 us
  Pallas kernels  47.1 us (96%)
  between operations  1.53 us (3%)
    pallas_call x1, Pallas kernels, attention(): pl.pallas_call(functools.partial(kernel, ['q', 'k', 'v', 'g', 'lists'] +...  46.3 us

profile of v8, /device:TPU:0, one launch (start us, length us, event | category | flops | bytes accessed | tf_op | source)
XLA Modules:
  0.0 48.9 jit_solution(4020600268010113509)
XLA Ops:
  0.6 0.0 copy-start
  0.6 0.0 copy-start.1
  0.7 0.0 copy-start.2
  0.7 0.0 copy-start.3
  0.7 0.0 copy-start.4
  0.7 46.3 %block_sparse_attention.1 = (bf16[256,128]{1,0:T(8,128)(2,1)S(1)}, bf16[256,128]{1,0:T(8,128)(2,1)S(1)}, bf16[256,128]{1,0:T(8,128)(2,1)S(1)}, bf16[256,128]{1,0:T(8,128)(2,1)S(1)}, f32[1,1]{1,0:T(1,128)}) custom-call(bf16[2,128,128]{2,1,0:T(8,128)(2,1)} %bitcast.10, bf16[2,128,128]{2,1,0:T(8,128)(2,1)} %bitcast.12, bf16[2,128,128]{2,1,0:T(8,128)(2,1)} %bitcast.14, ...), custom_call_target="tpu_custom_call" | custom-call | tf_op jit(solution)/shard_map/block_sparse_attention/pallas_call | solution.py:659
  47.7 0.0 copy-done
  47.7 0.0 copy-done.1
  47.7 0.0 copy-done.2
  47.7 0.0 copy-done.3
  47.7 0.0 copy-done.4
  47.7 1.0 %conditional.1 = ((bf16[256,128]{1,0:T(8,128)(2,1)}, bf16[256,128]{1,0:T(8,128)(2,1)}, bf16[256,128]{1,0:T(8,128)(2,1)}, bf16[256,128]{1,0:T(8,128)(2,1)})) conditional(s32[]{:T(128)} %bitcast.9, (bf16[256,128]{1,0:T(8,128)(2,1)S(1)}, bf16[256,128]{1,0:T(8,128)(2,1)S(1)}, bf16[256,128]{1,0:T(8,128)(2,1)S(1)}, ...), branch_computations={%region_0.0_spmd, %region_1.0_spmd} | conditional | bytes 8 | solution.py:698
  47.7 0.7 %hand_out.2 = (bf16[256,128]{1,0:T(8,128)(2,1)}, bf16[256,128]{1,0:T(8,128)(2,1)}, bf16[256,128]{1,0:T(8,128)(2,1)}, bf16[256,128]{1,0:T(8,128)(2,1)}) custom-call(bf16[256,128]{1,0:T(8,128)(2,1)S(1)} %get-tuple-element.18.refs_0_, bf16[256,128]{1,0:T(8,128)(2,1)S(1)} %get-tuple-element.19.refs_1_, bf16[256,128]{1,0:T(8,128)(2,1)S(1)} %get-tuple-element.20.refs_2_, ...), custom_call_target="tpu_custom_call" | custom-call | tf_op jit(solution)/shard_map/cond/branch_0_fun/hand_out/pallas_call | solution.py:684
Async XLA Ops:
  0.6 47.0 %copy-start = (bf16[256,128]{1,0:T(8,128)(2,1)S(1)}, bf16[256,128]{1,0:T(8,128)(2,1)}, u32[]{:S(2)}) copy-start(bf16[256,128]{1,0:T(8,128)(2,1)} %param.7) | copy-start | bytes 196612
  0.6 47.0 %copy-start.1 = (bf16[256,128]{1,0:T(8,128)(2,1)S(1)}, bf16[256,128]{1,0:T(8,128)(2,1)}, u32[]{:S(2)}) copy-start(bf16[256,128]{1,0:T(8,128)(2,1)} %param.8) | copy-start | bytes 196612
  0.7 47.0 %copy-start.2 = (bf16[256,128]{1,0:T(8,128)(2,1)S(1)}, bf16[256,128]{1,0:T(8,128)(2,1)}, u32[]{:S(2)}) copy-start(bf16[256,128]{1,0:T(8,128)(2,1)} %param.9) | copy-start | bytes 196612
  0.7 47.0 %copy-start.3 = (bf16[256,128]{1,0:T(8,128)(2,1)S(1)}, bf16[256,128]{1,0:T(8,128)(2,1)}, u32[]{:S(2)}) copy-start(bf16[256,128]{1,0:T(8,128)(2,1)} %param.10) | copy-start | bytes 196612
  0.7 47.0 %copy-start.4 = (s32[256,16]{0,1:T(8,128)S(1)}, s32[256,16]{0,1:T(8,128)}, u32[]{:S(2)}) copy-start(s32[256,16]{0,1:T(8,128)} %param.11) | copy-start | bytes 49156
